TPU v7x, 128 devices: a whole 4x4x4 slice. The times are simulated.
128 devices in a mesh: dp: 128 (over y, x, z, core).
Axes of the slice: x: 4, y: 4, z: 4, core: 2. Of those that a mesh axis runs over, the one named last changes fastest.
Arguments:
- teacher: bfloat16 [128, 128, 1536], P('dp'), may hold values from -24 to 24
- head_weight: bfloat16 [1536, 384], replicated, may hold values from -0.15625 to 0.15625
- neighbours: int32 [128, 6], replicated, may hold values from 0 to 127, as said below
Outputs:
- head_grad: float32 [1536, 384], P('dp')
- code_grad: float32 [128, 128, 384], P('dp')
Inputs may be any that keep to these rules, and one draw needn't show every extreme that they name: `neighbours`: each row names 6 different images, never its own index.
All inputs are finite; a program needn't handle non-finite values.
Results may differ from a plain program's by a relative error of at most 0.015.
Values may be sent and summed in bfloat16 or wider, within the bound.
A program may use at most 64 MiB of HBM per device.

v0:
```python
import jax
import jax.numpy as jnp
from jax import lax
from jax.sharding import PartitionSpec as P

EPS = 1e-06
LOSS_SCALE = 128.0
SHIFT_SELF = 0.18
WEIGHT_SELF = 0.1
SHIFT_PAIR = 0.12
WEIGHT_PAIR = 0.5


def unit_rows(features):
    values = features.astype(jnp.float32)
    return values * lax.rsqrt(jnp.sum(values * values, axis=-1, keepdims=True) + EPS)


def code_scale(codes):
    values = codes.astype(jnp.float32)
    return lax.rsqrt(jnp.sum(values * values, axis=-1, keepdims=True) + EPS)


def back_norm(grad, code_unit, inverse):
    values = code_unit.astype(jnp.float32)
    return (grad - values * jnp.sum(values * grad, axis=-1, keepdims=True)) * inverse


def body(teacher, head_weight, neighbours):
    count = lax.axis_size("dp")
    patches = teacher.shape[1]
    width = teacher.shape[2]
    code_width = head_weight.shape[1]
    rows = patches // count
    images = neighbours.shape[0]
    slots = neighbours.shape[1]
    own_unit = unit_rows(teacher[0]).astype(jnp.bfloat16)
    codes = jnp.dot(own_unit, head_weight, preferred_element_type=jnp.float32).astype(jnp.bfloat16)
    own_inv = code_scale(codes)
    own_code = (codes.astype(jnp.float32) * own_inv).astype(jnp.bfloat16)
    unit_pieces = own_unit.reshape(count, rows, width)
    held_units, held_codes = (
        lax.all_to_all(unit_pieces, "dp", split_axis=0, concat_axis=0, tiled=True),
        lax.all_to_all(
            codes.reshape(count, rows, code_width), "dp", split_axis=0, concat_axis=0, tiled=True
        ),
    )
    order = jnp.transpose(neighbours)
    send_units = held_units[order]
    tcorr_self = jnp.einsum("pd,qd->pq", own_unit, own_unit, preferred_element_type=jnp.float32)
    scor_self = jnp.einsum("pc,qc->pq", own_code, own_code, preferred_element_type=jnp.float32)
    gate_self = (
        -(LOSS_SCALE * WEIGHT_SELF) * (tcorr_self - SHIFT_SELF) * jnp.maximum(scor_self, 0.0)
    ).astype(jnp.bfloat16)
    grad_self = jnp.einsum("pq,qc->pc", gate_self, own_code, preferred_element_type=jnp.float32)
    grad_self = grad_self + jnp.einsum(
        "qp,qc->pc", gate_self, own_code, preferred_element_type=jnp.float32
    )
    partner_units = lax.all_to_all(send_units, "dp", split_axis=1, concat_axis=1, tiled=True)
    partner_codes = lax.all_to_all(held_codes[order], "dp", split_axis=1, concat_axis=1, tiled=True)
    items = partner_units.shape[0]
    finish_partner_units = partner_units.reshape(items, patches, width)
    finish_partner_codes = partner_codes.reshape(items, patches, code_width)
    partner_inv = code_scale(finish_partner_codes)
    partner_code = (finish_partner_codes.astype(jnp.float32) * partner_inv).astype(jnp.bfloat16)
    tcorr = jnp.einsum(
        "pd,nqd->npq", own_unit, finish_partner_units, preferred_element_type=jnp.float32
    )
    scor = jnp.einsum("pc,nqc->npq", own_code, partner_code, preferred_element_type=jnp.float32)
    gate = (-(LOSS_SCALE * WEIGHT_PAIR) * (tcorr - SHIFT_PAIR) * jnp.maximum(scor, 0.0)).astype(
        jnp.bfloat16
    )
    grads = jnp.einsum("npq,nqc->npc", gate, partner_code, preferred_element_type=jnp.float32)
    cross_raw = jnp.einsum("npq,pc->nqc", gate, own_code, preferred_element_type=jnp.float32)
    cross = back_norm(cross_raw, partner_code, partner_inv).astype(jnp.bfloat16)
    grads, cross = (grads, cross)
    grad_total = grad_self + jnp.sum(grads, axis=0)
    own_grad = back_norm(grad_total, own_code, own_inv)
    arrived = lax.all_to_all(
        cross.reshape(slots, count, rows, code_width), "dp", split_axis=1, concat_axis=1, tiled=True
    )
    targets = lax.broadcasted_iota(jnp.int32, (images, slots, images), 0)
    member = (order[None, :, :] == targets).astype(jnp.bfloat16)
    relayed = jnp.einsum(
        "jki,kirc->jrc", member, arrived, preferred_element_type=jnp.float32
    ).astype(jnp.bfloat16)
    collected = lax.all_to_all(relayed, "dp", split_axis=0, concat_axis=0, tiled=True)
    code_grad = own_grad + collected.reshape(patches, code_width).astype(jnp.float32)
    code_half = code_grad.astype(jnp.bfloat16)
    partial_grad = jnp.einsum("pd,pc->dc", own_unit, code_half, preferred_element_type=jnp.float32)
    head_grad = lax.psum_scatter(partial_grad, "dp", scatter_dimension=0, tiled=True)
    return (head_grad, code_grad[None])


def solution(mesh):
    return jax.shard_map(
        body,
        mesh=mesh,
        in_specs=(P("dp", None, None), P(), P()),
        out_specs=(P("dp", None), P("dp", None, None)),
        check_vma=False,
    )
```

profile of v0, /device:TPU:1, one launch (start us, length us, event | category | flops | bytes accessed | tf_op | source)
XLA Modules:
  0.0 583.7 jit_solution(18176388128246965167)
XLA Ops:
  0.6 1.7 copy_convert_fusion
  5.0 11.5 %all-to-all-start.2 = ((bf16[128,2,192]{2,1,0:T(2,128)(2,1)}), bf16[128,2,192]{2,1,0:T(2,128)(2,1)S(1)}, u32[]{:S(2)}, u32[]{:S(2)}) async-start(bf16[128,2,192]{2,1,0:T(2,128)(2,1)} %reshape.149), calls=%async_computation.2 | async-start | bytes 262144 | tf_op jit(solution)/shard_map/all_to_all | solution.py:44
  17.2 3.7 reduce
  20.9 1.8 reshape.147
  22.8 3.5 all-to-all-done.2
  27.0 6.2 %all-to-all-start = ((bf16[128,2,768]{2,1,0:T(2,128)(2,1)}), bf16[128,2,768]{2,1,0:T(2,128)(2,1)S(1)}, u32[]{:S(2)}, u32[]{:S(2)}) async-start(bf16[128,2,768]{2,1,0:T(2,128)(2,1)} %reshape.147), calls=%async_computation | async-start | bytes 786432 | tf_op jit(solution)/shard_map/all_to_all | solution.py:43
  34.4 2.6 gather_fusion.1
  38.2 7.2 %all-to-all-done = bf16[128,2,768]{2,1,0:T(2,128)(2,1)S(1)} async-done(((bf16[128,2,768]{2,1,0:T(2,128)(2,1)}), bf16[128,2,768]{2,1,0:T(2,128)(2,1)S(1)}, u32[]{:S(2)}, u32[]{:S(2)}) %all-to-all-start) | async-done | bytes 393248 | tf_op jit(solution)/shard_map/all_to_all | solution.py:43
  45.4 5.6 all-to-all-start.3
  53.3 3.8 gather_fusion
  57.1 4.6 copy.18
  61.7 5.5 all-to-all-done.3
  67.2 5.7 all-to-all-start.1
  73.9 1.3 fusion.16
  75.2 38.9 %all-to-all-done.1 = bf16[6,128,1,1536]{3,0,2,1:T(8,128)(2,1)} async-done(((bf16[6,128,1,1536]{3,0,2,1:T(8,128)(2,1)}), bf16[6,128,1,1536]{3,0,2,1:T(8,128)(2,1)}, u32[]{:S(2)}, u32[]{:S(2)}) %all-to-all-start.1) | async-done | bytes 2359328 | tf_op jit(solution)/shard_map/all_to_all | solution.py:59
  114.2 3.4 fusion.13
  117.6 1.5 fusion.20
  119.1 3.0 fusion.8
  123.4 4.7 all-to-all-start.4
  128.6 1.7 convolution_bitcast_fusion.1
  130.3 14.3 %all-to-all-done.4 = bf16[6,128,1,384]{3,0,2,1:T(8,128)(2,1)S(1)} async-done(((bf16[6,128,1,384]{3,0,2,1:T(8,128)(2,1)}), bf16[6,128,1,384]{3,0,2,1:T(8,128)(2,1)S(1)}, u32[]{:S(2)}, u32[]{:S(2)}) %all-to-all-start.4) | async-done | bytes 589856 | tf_op jit(solution)/shard_map/all_to_all | solution.py:79
  146.3 4.6 all-to-all-start.5
  151.3 9.6 %all-to-all-done.5 = bf16[128,2,192]{2,1,0:T(2,128)(2,1)S(1)} async-done(((bf16[128,2,192]{2,1,0:T(2,128)(2,1)}), bf16[128,2,192]{2,1,0:T(2,128)(2,1)S(1)}, u32[]{:S(2)}, u32[]{:S(2)}) %all-to-all-start.5) | async-done | bytes 98336 | tf_op jit(solution)/shard_map/all_to_all | solution.py:87
  161.1 2.0 fusion.53
  163.1 329.7 %fusion = f32[16,384]{1,0:T(8,128)S(1)} fusion(f32[1536,384]{1,0:T(8,128)} %fusion.53), kind=kCustom, calls=%all-reduce-scatter | all-reduce-scatter fusion | flops 786433 | bytes 2383872
  504.6 11.8 %collective-permute-start.22 = (f32[16,384]{1,0:T(8,128)S(1)}, f32[16,384]{1,0:T(8,128)S(1)}, u32[]{:S(2)}, u32[]{:S(2)}) collective-permute-start(f32[16,384]{1,0:T(8,128)S(1)} %fusion), channel_id=1, source_target_pairs={{0,23},{1,24},{2,25},{3,26},{4,27},{5,28},{6,29},{7,30},{8,31},{9,... | collective-permute-start | bytes 73736
  516.4 5.9 %collective-permute-start.21 = (f32[16,384]{1,0:T(8,128)S(1)}, f32[16,384]{1,0:T(8,128)S(1)}, u32[]{:S(2)}, u32[]{:S(2)}) collective-permute-start(f32[16,384]{1,0:T(8,128)S(1)} %fusion), channel_id=1, source_target_pairs={{0,22},{1,23},{2,24},{3,25},{4,26},{5,27},{6,28},{7,29},{8,30},{9,... | collective-permute-start | bytes 73736
  522.3 2.8 collective-permute-start.20
  525.2 2.2 collective-permute-start.19
  527.4 3.4 collective-permute-start.18
  530.8 3.1 collective-permute-start.17
  533.9 1.9 collective-permute-start.16
  535.9 1.9 collective-permute-start.15
  537.8 1.6 collective-permute-start.14
  539.4 1.8 collective-permute-start.13
  541.2 3.9 collective-permute-start.12
  545.1 3.4 collective-permute-start.11
  548.5 3.7 collective-permute-start.10
  553.6 2.1 collective-permute-start.8
  555.7 2.0 collective-permute-start.7
  557.7 2.8 collective-permute-start.6
  560.6 3.5 collective-permute-start.5
  564.0 2.7 collective-permute-start.4
  566.8 3.0 collective-permute-start.3
  569.8 3.5 collective-permute-start.2
  573.4 2.2 collective-permute-start.1
  575.6 2.8 collective-permute-start
  579.3 3.8 concatenate
  (81 shorter events, 28.0 us)
Async XLA Ops:
  0.6 1.9 copy-start
  2.5 14.0 %copy-start.1 = (bf16[1,128,1536]{2,1,0:T(8,128)(2,1)S(1)}, bf16[1,128,1536]{2,1,0:T(8,128)(2,1)}, u32[]{:S(2)}) copy-start(bf16[1,128,1536]{2,1,0:T(8,128)(2,1)} %param.3) | copy-start | bytes 1179652
  5.0 21.3 %all-to-all-start.2 = ((bf16[128,2,192]{2,1,0:T(2,128)(2,1)}), bf16[128,2,192]{2,1,0:T(2,128)(2,1)S(1)}, u32[]{:S(2)}, u32[]{:S(2)}) async-start(bf16[128,2,192]{2,1,0:T(2,128)(2,1)} %reshape.149), calls=%async_computation.2 | async-start | bytes 262144 | tf_op jit(solution)/shard_map/all_to_all | solution.py:44
  17.2 16.0 %copy-start.3 = (s32[128,6]{0,1:T(8,128)S(1)}, s32[128,6]{0,1:T(8,128)}, u32[]{:S(2)}) copy-start(s32[128,6]{0,1:T(8,128)} %param.5) | copy-start | bytes 9220
  26.3 0.7 copy-start.2
  27.0 18.4 %all-to-all-start = ((bf16[128,2,768]{2,1,0:T(2,128)(2,1)}), bf16[128,2,768]{2,1,0:T(2,128)(2,1)S(1)}, u32[]{:S(2)}, u32[]{:S(2)}) async-start(bf16[128,2,768]{2,1,0:T(2,128)(2,1)} %reshape.147), calls=%async_computation | async-start | bytes 786432 | tf_op jit(solution)/shard_map/all_to_all | solution.py:43
  45.4 21.8 %all-to-all-start.3 = ((bf16[6,128,1,384]{3,0,2,1:T(8,128)(2,1)}), bf16[6,128,1,384]{3,0,2,1:T(8,128)(2,1)}, u32[]{:S(2)}, u32[]{:S(2)}) async-start(bf16[6,128,1,384]{3,0,2,1:T(8,128)(2,1)} %copy.21), calls=%async_computation.3 | async-start | bytes 1572864 | tf_op jit(solution)/shard_map/all_to_all | solution.py:60
  67.2 47.0 %all-to-all-start.1 = ((bf16[6,128,1,1536]{3,0,2,1:T(8,128)(2,1)}), bf16[6,128,1,1536]{3,0,2,1:T(8,128)(2,1)}, u32[]{:S(2)}, u32[]{:S(2)}) async-start(bf16[6,128,1,1536]{3,0,2,1:T(8,128)(2,1)} %copy.18), calls=%async_computation.1 | async-start | bytes 6291456 | tf_op jit(solution)/shard_map/all_to_all | solution.py:59
  119.1 3.0 copy-start.4
  123.4 21.2 %all-to-all-start.4 = ((bf16[6,128,1,384]{3,0,2,1:T(8,128)(2,1)}), bf16[6,128,1,384]{3,0,2,1:T(8,128)(2,1)S(1)}, u32[]{:S(2)}, u32[]{:S(2)}) async-start(bf16[6,128,1,384]{3,0,2,1:T(8,128)(2,1)} %copy.24), calls=%async_computation.4 | async-start | bytes 1572864 | tf_op jit(solution)/shard_map/all_to_all | solution.py:79
  146.3 14.6 %all-to-all-start.5 = ((bf16[128,2,192]{2,1,0:T(2,128)(2,1)}), bf16[128,2,192]{2,1,0:T(2,128)(2,1)S(1)}, u32[]{:S(2)}, u32[]{:S(2)}) async-start(bf16[128,2,192]{2,1,0:T(2,128)(2,1)} %reshape.151), calls=%async_computation.5 | async-start | bytes 262144 | tf_op jit(solution)/shard_map/all_to_all | solution.py:87
  492.8 7.8 %collective-permute-start.30 = (f32[16,384]{1,0:T(8,128)S(1)}, f32[16,384]{1,0:T(8,128)S(1)}, u32[]{:S(2)}, u32[]{:S(2)}) collective-permute-start(f32[16,384]{1,0:T(8,128)S(1)} %fusion), channel_id=1, source_target_pairs={{0,31},{1,32},{2,33},{3,34},{4,35},{5,36},{6,37},{7,38},{8,39},{9,... | collective-permute-start | bytes 73736
  494.1 5.2 collective-permute-start.31
  495.4 6.5 %collective-permute-start.29 = (f32[16,384]{1,0:T(8,128)S(1)}, f32[16,384]{1,0:T(8,128)S(1)}, u32[]{:S(2)}, u32[]{:S(2)}) collective-permute-start(f32[16,384]{1,0:T(8,128)S(1)} %fusion), channel_id=1, source_target_pairs={{0,30},{1,31},{2,32},{3,33},{4,34},{5,35},{6,36},{7,37},{8,38},{9,... | collective-permute-start | bytes 73736
  496.7 6.5 %collective-permute-start.28 = (f32[16,384]{1,0:T(8,128)S(1)}, f32[16,384]{1,0:T(8,128)S(1)}, u32[]{:S(2)}, u32[]{:S(2)}) collective-permute-start(f32[16,384]{1,0:T(8,128)S(1)} %fusion), channel_id=1, source_target_pairs={{0,29},{1,30},{2,31},{3,32},{4,33},{5,34},{6,35},{7,36},{8,37},{9,... | collective-permute-start | bytes 73736
  498.0 6.5 %collective-permute-start.27 = (f32[16,384]{1,0:T(8,128)S(1)}, f32[16,384]{1,0:T(8,128)S(1)}, u32[]{:S(2)}, u32[]{:S(2)}) collective-permute-start(f32[16,384]{1,0:T(8,128)S(1)} %fusion), channel_id=1, source_target_pairs={{0,28},{1,29},{2,30},{3,31},{4,32},{5,33},{6,34},{7,35},{8,36},{9,... | collective-permute-start | bytes 73736
  499.3 17.1 %collective-permute-start.26 = (f32[16,384]{1,0:T(8,128)S(1)}, f32[16,384]{1,0:T(8,128)S(1)}, u32[]{:S(2)}, u32[]{:S(2)}) collective-permute-start(f32[16,384]{1,0:T(8,128)S(1)} %fusion), channel_id=1, source_target_pairs={{0,27},{1,28},{2,29},{3,30},{4,31},{5,32},{6,33},{7,34},{8,35},{9,... | collective-permute-start | bytes 73736
  500.6 21.7 %collective-permute-start.25 = (f32[16,384]{1,0:T(8,128)S(1)}, f32[16,384]{1,0:T(8,128)S(1)}, u32[]{:S(2)}, u32[]{:S(2)}) collective-permute-start(f32[16,384]{1,0:T(8,128)S(1)} %fusion), channel_id=1, source_target_pairs={{0,26},{1,27},{2,28},{3,29},{4,30},{5,31},{6,32},{7,33},{8,34},{9,... | collective-permute-start | bytes 73736
  501.9 23.2 %collective-permute-start.24 = (f32[16,384]{1,0:T(8,128)S(1)}, f32[16,384]{1,0:T(8,128)S(1)}, u32[]{:S(2)}, u32[]{:S(2)}) collective-permute-start(f32[16,384]{1,0:T(8,128)S(1)} %fusion), channel_id=1, source_target_pairs={{0,25},{1,26},{2,27},{3,28},{4,29},{5,30},{6,31},{7,32},{8,33},{9,... | collective-permute-start | bytes 73736
  503.2 24.2 %collective-permute-start.23 = (f32[16,384]{1,0:T(8,128)S(1)}, f32[16,384]{1,0:T(8,128)S(1)}, u32[]{:S(2)}, u32[]{:S(2)}) collective-permute-start(f32[16,384]{1,0:T(8,128)S(1)} %fusion), channel_id=1, source_target_pairs={{0,24},{1,25},{2,26},{3,27},{4,28},{5,29},{6,30},{7,31},{8,32},{9,... | collective-permute-start | bytes 73736
  504.6 26.3 %collective-permute-start.22 = (f32[16,384]{1,0:T(8,128)S(1)}, f32[16,384]{1,0:T(8,128)S(1)}, u32[]{:S(2)}, u32[]{:S(2)}) collective-permute-start(f32[16,384]{1,0:T(8,128)S(1)} %fusion), channel_id=1, source_target_pairs={{0,23},{1,24},{2,25},{3,26},{4,27},{5,28},{6,29},{7,30},{8,31},{9,... | collective-permute-start | bytes 73736
  516.4 17.5 %collective-permute-start.21 = (f32[16,384]{1,0:T(8,128)S(1)}, f32[16,384]{1,0:T(8,128)S(1)}, u32[]{:S(2)}, u32[]{:S(2)}) collective-permute-start(f32[16,384]{1,0:T(8,128)S(1)} %fusion), channel_id=1, source_target_pairs={{0,22},{1,23},{2,24},{3,25},{4,26},{5,27},{6,28},{7,29},{8,30},{9,... | collective-permute-start | bytes 73736
  522.3 13.6 %collective-permute-start.20 = (f32[16,384]{1,0:T(8,128)S(1)}, f32[16,384]{1,0:T(8,128)S(1)}, u32[]{:S(2)}, u32[]{:S(2)}) collective-permute-start(f32[16,384]{1,0:T(8,128)S(1)} %fusion), channel_id=1, source_target_pairs={{0,21},{1,22},{2,23},{3,24},{4,25},{5,26},{6,27},{7,28},{8,29},{9,... | collective-permute-start | bytes 73736
  525.2 12.7 %collective-permute-start.19 = (f32[16,384]{1,0:T(8,128)S(1)}, f32[16,384]{1,0:T(8,128)S(1)}, u32[]{:S(2)}, u32[]{:S(2)}) collective-permute-start(f32[16,384]{1,0:T(8,128)S(1)} %fusion), channel_id=1, source_target_pairs={{0,20},{1,21},{2,22},{3,23},{4,24},{5,25},{6,26},{7,27},{8,28},{9,... | collective-permute-start | bytes 73736
  527.4 12.0 %collective-permute-start.18 = (f32[16,384]{1,0:T(8,128)S(1)}, f32[16,384]{1,0:T(8,128)S(1)}, u32[]{:S(2)}, u32[]{:S(2)}) collective-permute-start(f32[16,384]{1,0:T(8,128)S(1)} %fusion), channel_id=1, source_target_pairs={{0,19},{1,20},{2,21},{3,22},{4,23},{5,24},{6,25},{7,26},{8,27},{9,... | collective-permute-start | bytes 73736
  530.8 10.4 %collective-permute-start.17 = (f32[16,384]{1,0:T(8,128)S(1)}, f32[16,384]{1,0:T(8,128)S(1)}, u32[]{:S(2)}, u32[]{:S(2)}) collective-permute-start(f32[16,384]{1,0:T(8,128)S(1)} %fusion), channel_id=1, source_target_pairs={{0,18},{1,19},{2,20},{3,21},{4,22},{5,23},{6,24},{7,25},{8,26},{9,... | collective-permute-start | bytes 73736
  533.9 11.2 %collective-permute-start.16 = (f32[16,384]{1,0:T(8,128)S(1)}, f32[16,384]{1,0:T(8,128)S(1)}, u32[]{:S(2)}, u32[]{:S(2)}) collective-permute-start(f32[16,384]{1,0:T(8,128)S(1)} %fusion), channel_id=1, source_target_pairs={{0,17},{1,18},{2,19},{3,20},{4,21},{5,22},{6,23},{7,24},{8,25},{9,... | collective-permute-start | bytes 73736
  535.9 12.6 %collective-permute-start.15 = (f32[16,384]{1,0:T(8,128)S(1)}, f32[16,384]{1,0:T(8,128)S(1)}, u32[]{:S(2)}, u32[]{:S(2)}) collective-permute-start(f32[16,384]{1,0:T(8,128)S(1)} %fusion), channel_id=1, source_target_pairs={{0,16},{1,17},{2,18},{3,19},{4,20},{5,21},{6,22},{7,23},{8,24},{9,... | collective-permute-start | bytes 73736
  537.8 14.5 %collective-permute-start.14 = (f32[16,384]{1,0:T(8,128)S(1)}, f32[16,384]{1,0:T(8,128)S(1)}, u32[]{:S(2)}, u32[]{:S(2)}) collective-permute-start(f32[16,384]{1,0:T(8,128)S(1)} %fusion), channel_id=1, source_target_pairs={{0,15},{1,16},{2,17},{3,18},{4,19},{5,20},{6,21},{7,22},{8,23},{9,... | collective-permute-start | bytes 73736
  539.4 14.2 %collective-permute-start.13 = (f32[16,384]{1,0:T(8,128)S(1)}, f32[16,384]{1,0:T(8,128)S(1)}, u32[]{:S(2)}, u32[]{:S(2)}) collective-permute-start(f32[16,384]{1,0:T(8,128)S(1)} %fusion), channel_id=1, source_target_pairs={{0,14},{1,15},{2,16},{3,17},{4,18},{5,19},{6,20},{7,21},{8,22},{9,... | collective-permute-start | bytes 73736
  541.2 14.4 %collective-permute-start.12 = (f32[16,384]{1,0:T(8,128)S(1)}, f32[16,384]{1,0:T(8,128)S(1)}, u32[]{:S(2)}, u32[]{:S(2)}) collective-permute-start(f32[16,384]{1,0:T(8,128)S(1)} %fusion), channel_id=1, source_target_pairs={{0,13},{1,14},{2,15},{3,16},{4,17},{5,18},{6,19},{7,20},{8,21},{9,... | collective-permute-start | bytes 73736
  545.1 12.6 %collective-permute-start.11 = (f32[16,384]{1,0:T(8,128)S(1)}, f32[16,384]{1,0:T(8,128)S(1)}, u32[]{:S(2)}, u32[]{:S(2)}) collective-permute-start(f32[16,384]{1,0:T(8,128)S(1)} %fusion), channel_id=1, source_target_pairs={{0,12},{1,13},{2,14},{3,15},{4,16},{5,17},{6,18},{7,19},{8,20},{9,... | collective-permute-start | bytes 73736
  548.5 12.0 %collective-permute-start.10 = (f32[16,384]{1,0:T(8,128)S(1)}, f32[16,384]{1,0:T(8,128)S(1)}, u32[]{:S(2)}, u32[]{:S(2)}) collective-permute-start(f32[16,384]{1,0:T(8,128)S(1)} %fusion), channel_id=1, source_target_pairs={{0,11},{1,12},{2,13},{3,14},{4,15},{5,16},{6,17},{7,18},{8,19},{9,... | collective-permute-start | bytes 73736
  552.3 11.7 %collective-permute-start.9 = (f32[16,384]{1,0:T(8,128)S(1)}, f32[16,384]{1,0:T(8,128)S(1)}, u32[]{:S(2)}, u32[]{:S(2)}) collective-permute-start(f32[16,384]{1,0:T(8,128)S(1)} %fusion), channel_id=1, source_target_pairs={{0,10},{1,11},{2,12},{3,13},{4,14},{5,15},{6,16},{7,17},{8,18},{9,... | collective-permute-start | bytes 73736
  553.6 13.2 %collective-permute-start.8 = (f32[16,384]{1,0:T(8,128)S(1)}, f32[16,384]{1,0:T(8,128)S(1)}, u32[]{:S(2)}, u32[]{:S(2)}) collective-permute-start(f32[16,384]{1,0:T(8,128)S(1)} %fusion), channel_id=1, source_target_pairs={{0,9},{1,10},{2,11},{3,12},{4,13},{5,14},{6,15},{7,16},{8,17},{9,1... | collective-permute-start | bytes 73736
  555.7 14.1 %collective-permute-start.7 = (f32[16,384]{1,0:T(8,128)S(1)}, f32[16,384]{1,0:T(8,128)S(1)}, u32[]{:S(2)}, u32[]{:S(2)}) collective-permute-start(f32[16,384]{1,0:T(8,128)S(1)} %fusion), channel_id=1, source_target_pairs={{0,8},{1,9},{2,10},{3,11},{4,12},{5,13},{6,14},{7,15},{8,16},{9,17... | collective-permute-start | bytes 73736
  557.7 15.6 %collective-permute-start.6 = (f32[16,384]{1,0:T(8,128)S(1)}, f32[16,384]{1,0:T(8,128)S(1)}, u32[]{:S(2)}, u32[]{:S(2)}) collective-permute-start(f32[16,384]{1,0:T(8,128)S(1)} %fusion), channel_id=1, source_target_pairs={{0,7},{1,8},{2,9},{3,10},{4,11},{5,12},{6,13},{7,14},{8,15},{9,16}... | collective-permute-start | bytes 73736
  560.6 15.0 %collective-permute-start.5 = (f32[16,384]{1,0:T(8,128)S(1)}, f32[16,384]{1,0:T(8,128)S(1)}, u32[]{:S(2)}, u32[]{:S(2)}) collective-permute-start(f32[16,384]{1,0:T(8,128)S(1)} %fusion), channel_id=1, source_target_pairs={{0,6},{1,7},{2,8},{3,9},{4,10},{5,11},{6,12},{7,13},{8,14},{9,15},... | collective-permute-start | bytes 73736
  564.0 15.1 %collective-permute-start.4 = (f32[16,384]{1,0:T(8,128)S(1)}, f32[16,384]{1,0:T(8,128)S(1)}, u32[]{:S(2)}, u32[]{:S(2)}) collective-permute-start(f32[16,384]{1,0:T(8,128)S(1)} %fusion), channel_id=1, source_target_pairs={{0,5},{1,6},{2,7},{3,8},{4,9},{5,10},{6,11},{7,12},{8,13},{9,14},{... | collective-permute-start | bytes 73736
  566.8 12.4 %collective-permute-start.3 = (f32[16,384]{1,0:T(8,128)S(1)}, f32[16,384]{1,0:T(8,128)S(1)}, u32[]{:S(2)}, u32[]{:S(2)}) collective-permute-start(f32[16,384]{1,0:T(8,128)S(1)} %fusion), channel_id=1, source_target_pairs={{0,4},{1,5},{2,6},{3,7},{4,8},{5,9},{6,10},{7,11},{8,12},{9,13},{1... | collective-permute-start | bytes 73736
  569.8 9.3 %collective-permute-start.2 = (f32[16,384]{1,0:T(8,128)S(1)}, f32[16,384]{1,0:T(8,128)S(1)}, u32[]{:S(2)}, u32[]{:S(2)}) collective-permute-start(f32[16,384]{1,0:T(8,128)S(1)} %fusion), channel_id=1, source_target_pairs={{0,3},{1,4},{2,5},{3,6},{4,7},{5,8},{6,9},{7,10},{8,11},{9,12},{10... | collective-permute-start | bytes 73736
  573.4 5.8 collective-permute-start.1
  575.6 3.7 collective-permute-start
where the time goes:
time: 586 us; the launch traced here: 584 us
  blocking collectives  330 us (56%)
  starting transfers between devices  123 us (21%)
  waiting for transfers between devices  79.3 us (14%)
  local copies, waits for them, and re-layouts  26.1 us (4%)
  matrix products  13.4 us (2%)
  other arithmetic  10.4 us (2%)
    unnamed x1, blocking collectives  330 us
    unnamed x32, starting transfers between devices  85 us
    all_to_all x1, waiting for transfers between devices, body(): lax.all_to_all(send_units, 'dp', split_axis=1, concat_axis=1, tiled=True)  38.9 us
    all_to_all x1, waiting for transfers between devices, body(): lax.all_to_all(cross.reshape(slots, count, rows, code_width), 'dp', split...  14.3 us
    unnamed x21, local copies, waits for them, and re-layouts  12 us
  transfers between devices with their start and end apart: 38, of which 7 were waited for; matrix products, arithmetic and copies ran while one was open for 5% of the time, Pallas kernels for 0%

commit v1 on v0

--- a/solution.py
+++ b/solution.py
@@ -39,12 +39,7 @@
     own_inv = code_scale(codes)
     own_code = (codes.astype(jnp.float32) * own_inv).astype(jnp.bfloat16)
     unit_pieces = own_unit.reshape(count, rows, width)
-    held_units, held_codes = (
-        lax.all_to_all(unit_pieces, "dp", split_axis=0, concat_axis=0, tiled=True),
-        lax.all_to_all(
-            codes.reshape(count, rows, code_width), "dp", split_axis=0, concat_axis=0, tiled=True
-        ),
-    )
+    held_units = lax.all_to_all(unit_pieces, "dp", split_axis=0, concat_axis=0, tiled=True)
     order = jnp.transpose(neighbours)
     send_units = held_units[order]
     tcorr_self = jnp.einsum("pd,qd->pq", own_unit, own_unit, preferred_element_type=jnp.float32)
@@ -57,10 +52,11 @@
         "qp,qc->pc", gate_self, own_code, preferred_element_type=jnp.float32
     )
     partner_units = lax.all_to_all(send_units, "dp", split_axis=1, concat_axis=1, tiled=True)
-    partner_codes = lax.all_to_all(held_codes[order], "dp", split_axis=1, concat_axis=1, tiled=True)
     items = partner_units.shape[0]
     finish_partner_units = partner_units.reshape(items, patches, width)
-    finish_partner_codes = partner_codes.reshape(items, patches, code_width)
+    finish_partner_codes = jnp.einsum(
+        "nqd,dc->nqc", finish_partner_units, head_weight, preferred_element_type=jnp.float32
+    ).astype(jnp.bfloat16)
     partner_inv = code_scale(finish_partner_codes)
     partner_code = (finish_partner_codes.astype(jnp.float32) * partner_inv).astype(jnp.bfloat16)
     tcorr = jnp.einsum(
@@ -88,7 +84,9 @@
     code_grad = own_grad + collected.reshape(patches, code_width).astype(jnp.float32)
     code_half = code_grad.astype(jnp.bfloat16)
     partial_grad = jnp.einsum("pd,pc->dc", own_unit, code_half, preferred_element_type=jnp.float32)
-    head_grad = lax.psum_scatter(partial_grad, "dp", scatter_dimension=0, tiled=True)
+    shares = partial_grad.astype(jnp.bfloat16).reshape(count, width // count, code_width)
+    arrived_shares = lax.all_to_all(shares, "dp", split_axis=0, concat_axis=0, tiled=True)
+    head_grad = jnp.sum(arrived_shares.astype(jnp.float32), axis=0)
     return (head_grad, code_grad[None])
 
 

time: 586 us -> 169 us (0.29)
  blocking collectives: 330 us -> 0 us
  starting transfers between devices: 123 us -> 31 us
  waiting for transfers between devices: 79.3 us -> 98.3 us
  local copies, waits for them, and re-layouts: 26.1 us -> 14.4 us
    unnamed x1 -> x0, blocking collectives: 330 us -> none
    unnamed x32 -> x0, starting transfers between devices: 85 us -> none
    all_to_all x2 -> x1, waiting for transfers between devices: 9.03 us -> 24 us  [body(): lax.all_to_all(shares, 'dp', split_axis=0, concat_axis=0, tiled=True)]
    all_to_all x2 -> x1, starting transfers between devices: 17.1 us -> 4.45 us  [body(): lax.all_to_all(shares, 'dp', split_axis=0, concat_axis=0, tiled=True)]
    unnamed x21 -> x29, local copies, waits for them, and re-layouts: 12 us -> 2.9 us
  transfers between devices with their start and end apart: 38 -> 5, of which waited for: 7 -> 5; matrix products, arithmetic and copies ran while one was open for 5% -> 4% of each run, Pallas kernels for 0% -> 0%
where the time goes in v1:
time: 169 us
  waiting for transfers between devices  98.3 us (58%)
  starting transfers between devices  31 us (18%)
  matrix products  15.2 us (9%)
  local copies, waits for them, and re-layouts  14.4 us (9%)
  other arithmetic  8.71 us (5%)
    all_to_all x1, waiting for transfers between devices, body(): lax.all_to_all(send_units, 'dp', split_axis=1, concat_axis=1, tiled=True)  39.1 us
    all_to_all x1, waiting for transfers between devices, body(): lax.all_to_all(shares, 'dp', split_axis=0, concat_axis=0, tiled=True)  24 us
    all_to_all x1, waiting for transfers between devices, body(): lax.all_to_all(cross.reshape(slots, count, rows, code_width), 'dp', split...  13.4 us
    all_to_all x1, waiting for transfers between devices, body(): lax.all_to_all(unit_pieces, 'dp', split_axis=0, concat_axis=0, tiled=True)  12.2 us
    all_to_all x1, starting transfers between devices, body(): lax.all_to_all(unit_pieces, 'dp', split_axis=0, concat_axis=0, tiled=True)  11.5 us
    all_to_all x1, waiting for transfers between devices, body(): lax.all_to_all(relayed, 'dp', split_axis=0, concat_axis=0, tiled=True)  9.64 us
    gather x2, local copies, waits for them, and re-layouts, body(): send_units = held_units[order]  8.44 us
    all_to_all x1, starting transfers between devices, body(): lax.all_to_all(send_units, 'dp', split_axis=1, concat_axis=1, tiled=True)  5.68 us
  transfers between devices with their start and end apart: 5, of which 5 were waited for; matrix products, arithmetic and copies ran while one was open for 4% of the time, Pallas kernels for 0%

profile of v1, /device:TPU:1, one launch (start us, length us, event | category | flops | bytes accessed | tf_op | source)
XLA Modules:
  0.0 168.5 jit_solution(5408340169648205035)
XLA Ops:
  0.6 0.0 copy-start
  0.6 0.0 copy-start.1
  0.7 1.7 %copy_convert_fusion = f32[1,128,1536]{2,0,1:T(1,128)S(1)} fusion(bf16[1,128,1536]{2,1,0:T(8,128)(2,1)} %param.3), kind=kLoop, calls=%fused_computation.48 | loop fusion | flops 196608 | bytes 1179648 | tf_op jit(solution)/shard_map/convert_element_type | solution.py:15
  2.4 0.1 fusion.34
  2.5 0.7 fusion.36
  3.2 0.5 broadcast.69
  3.7 3.0 %reduce = bf16[128,1536]{1,0:T(8,128)(2,1)S(1)} reduce(bf16[128,1,1536]{2,1,0:T(2,128)(2,1)S(1)} %fusion.36, bf16[]{:T(256)} %broadcast.69), dimensions={1}, to_apply=%fusion.36.reduce_sub_computation | reduce | bytes 786434 | tf_op jit(solution)/shard_map/convert_element_type | solution.py:37
  6.7 0.8 reshape.131
  7.6 11.5 %all-to-all-start = ((bf16[128,2,768]{2,1,0:T(2,128)(2,1)}), bf16[128,2,768]{2,1,0:T(2,128)(2,1)S(1)}, u32[]{:S(2)}, u32[]{:S(2)}) async-start(bf16[128,2,768]{2,1,0:T(2,128)(2,1)} %reshape.131), calls=%async_computation | async-start | bytes 786432 | tf_op jit(solution)/shard_map/all_to_all | solution.py:42
  19.1 12.2 %all-to-all-done = bf16[128,2,768]{2,1,0:T(2,128)(2,1)S(1)} async-done(((bf16[128,2,768]{2,1,0:T(2,128)(2,1)}), bf16[128,2,768]{2,1,0:T(2,128)(2,1)S(1)}, u32[]{:S(2)}, u32[]{:S(2)}) %all-to-all-start) | async-done | bytes 393248 | tf_op jit(solution)/shard_map/all_to_all | solution.py:42
  31.3 0.3 reshape.132
  31.6 0.1 copy.74
  31.7 3.8 %gather_fusion = bf16[768,1536]{1,0:T(8,128)(2,1)} fusion(bf16[128,1536]{1,0:T(8,128)(2,1)S(1)} %bitcast.95, s32[1024]{0:T(1024)S(1)} %pad_clamp_fusion), kind=kCustom, calls=%fused_computation | custom fusion | bytes 4721664 | tf_op jit(solution)/shard_map/gather | solution.py:44
  35.5 4.6 %copy.16 = bf16[6,128,1,1536]{3,0,2,1:T(8,128)(2,1)} copy(bf16[6,128,1,1536]{3,1,0,2:T(8,128)(2,1)} %bitcast.96) | data formatting | bytes 4718592 | tf_op jit(solution)/shard_map/gather | solution.py:44
  40.1 5.7 %all-to-all-start.1 = ((bf16[6,128,1,1536]{3,0,2,1:T(8,128)(2,1)}), bf16[6,128,1,1536]{3,0,2,1:T(8,128)(2,1)}, u32[]{:S(2)}, u32[]{:S(2)}) async-start(bf16[6,128,1,1536]{3,0,2,1:T(8,128)(2,1)} %copy.16), calls=%async_computation.1 | async-start | bytes 6291456 | tf_op jit(solution)/shard_map/all_to_all | solution.py:54
  45.8 0.5 multiply_reduce_fusion
  46.3 0.1 multiply_convert_fusion.1
  46.4 0.7 multiply_convert_fusion
  47.1 0.9 fusion.31
  48.0 39.1 %all-to-all-done.1 = bf16[6,128,1,1536]{3,0,2,1:T(8,128)(2,1)} async-done(((bf16[6,128,1,1536]{3,0,2,1:T(8,128)(2,1)}), bf16[6,128,1,1536]{3,0,2,1:T(8,128)(2,1)}, u32[]{:S(2)}, u32[]{:S(2)}) %all-to-all-start.1) | async-done | bytes 2359328 | tf_op jit(solution)/shard_map/all_to_all | solution.py:54
  87.0 3.4 %fusion.21 = (f32[6,128]{1,0:T(8,128)S(1)}, bf16[6,128,384]{2,1,0:T(8,128)(2,1)S(1)}) fusion(bf16[1536,384]{1,0:T(8,128)(2,1)S(1)} %copy-done, bf16[6,128,1,1536]{3,0,2,1:T(8,128)(2,1)} %all-to-all-done.1), kind=kOutput, calls=%fused_computation.23 | convolution fusion | flops 907148544 | bytes 4131840 | tf_op jit(solution)/shard_map/nqd,dc->nqc/dot_general | solution.py:57
  90.4 3.5 %fusion.18 = f32[6,128,128]{2,1,0:T(8,128)S(1)} fusion(bf16[6,128,1,1536]{3,0,2,1:T(8,128)(2,1)} %all-to-all-done.1, bf16[1,128,1536]{2,0,1:T(2,128)(2,1)S(1)} %multiply_convert_fusion), kind=kOutput, calls=%fused_computation.22 | convolution fusion | flops 302186496 | bytes 3145728 | tf_op jit(solution)/shard_map/pd,nqd->npq/dot_general | solution.py:62
  93.9 0.4 fusion.26
  94.3 0.0 copy-start.8
  94.3 1.5 fusion.13
  95.8 0.0 copy-done.8
  95.8 1.2 copy.19
  97.1 4.7 %all-to-all-start.2 = ((bf16[6,128,1,384]{3,0,2,1:T(8,128)(2,1)}), bf16[6,128,1,384]{3,0,2,1:T(8,128)(2,1)S(1)}, u32[]{:S(2)}, u32[]{:S(2)}) async-start(bf16[6,128,1,384]{3,0,2,1:T(8,128)(2,1)} %copy.19), calls=%async_computation.2 | async-start | bytes 1572864 | tf_op jit(solution)/shard_map/all_to_all | solution.py:75
  101.8 0.2 fusion.32
  102.0 0.9 fusion.67
  102.9 2.0 %convolution_bitcast_fusion.1 = f32[128,384]{1,0:T(8,128)} fusion(bf16[6,128,128]{1,2,0:T(8,128)(2,1)} %copy-done.8, bf16[6,128,384]{2,1,0:T(8,128)(2,1)S(1)} %get-tuple-element.3, f32[6,128]{1,0:T(8,128)S(1)} %add_rsqrt_fusion), kind=kOutput, calls=%fused_computation.30 | convolution fusion | flops 76382208 | bytes 986112 | tf_op jit(solution)/shard_map/npq,nqc->npc/dot_general | solution.py:69
  104.9 13.4 %all-to-all-done.2 = bf16[6,128,1,384]{3,0,2,1:T(8,128)(2,1)S(1)} async-done(((bf16[6,128,1,384]{3,0,2,1:T(8,128)(2,1)}), bf16[6,128,1,384]{3,0,2,1:T(8,128)(2,1)S(1)}, u32[]{:S(2)}, u32[]{:S(2)}) %all-to-all-start.2) | async-done | bytes 589856 | tf_op jit(solution)/shard_map/all_to_all | solution.py:75
  118.3 0.3 fusion.29
  118.6 0.7 reduce.1
  119.2 0.8 reshape.133
  120.0 4.6 %all-to-all-start.3 = ((bf16[128,2,192]{2,1,0:T(2,128)(2,1)}), bf16[128,2,192]{2,1,0:T(2,128)(2,1)S(1)}, u32[]{:S(2)}, u32[]{:S(2)}) async-start(bf16[128,2,192]{2,1,0:T(2,128)(2,1)} %reshape.133), calls=%async_computation.3 | async-start | bytes 262144 | tf_op jit(solution)/shard_map/all_to_all | solution.py:83
  124.7 0.3 fusion.44
  125.0 9.6 %all-to-all-done.3 = bf16[128,2,192]{2,1,0:T(2,128)(2,1)S(1)} async-done(((bf16[128,2,192]{2,1,0:T(2,128)(2,1)}), bf16[128,2,192]{2,1,0:T(2,128)(2,1)S(1)}, u32[]{:S(2)}, u32[]{:S(2)}) %all-to-all-start.3) | async-done | bytes 98336 | tf_op jit(solution)/shard_map/all_to_all | solution.py:83
  134.6 0.9 reshape.134
  135.5 1.5 convolution_convert_fusion
  137.0 1.3 reshape.108
  138.3 4.4 %all-to-all-start.4 = ((bf16[128,12,384]{2,1,0:T(8,128)(2,1)}), bf16[128,12,384]{2,1,0:T(8,128)(2,1)S(1)}, u32[]{:S(2)}, u32[]{:S(2)}) async-start(bf16[128,12,384]{2,1,0:T(8,128)(2,1)} %reshape.108), calls=%async_computation.4 | async-start | bytes 3145728 | tf_op jit(solution)/shard_map/all_to_all | solution.py:88
  142.8 0.0 copy-done.3
  142.8 0.0 copy-done.5
  142.8 0.0 copy-done.6
  142.8 0.8 fusion.65
  143.6 24.0 %all-to-all-done.4 = bf16[128,12,384]{2,1,0:T(8,128)(2,1)S(1)} async-done(((bf16[128,12,384]{2,1,0:T(8,128)(2,1)}), bf16[128,12,384]{2,1,0:T(8,128)(2,1)S(1)}, u32[]{:S(2)}, u32[]{:S(2)}) %all-to-all-start.4) | async-done | bytes 1179680 | tf_op jit(solution)/shard_map/all_to_all | solution.py:88
  167.6 0.9 convert_reduce_fusion
  (22 shorter events, 0.1 us)
Async XLA Ops:
  0.6 45.2 %copy-start = (bf16[1536,384]{1,0:T(8,128)(2,1)S(1)}, bf16[1536,384]{1,0:T(8,128)(2,1)}, u32[]{:S(2)}) copy-start(bf16[1536,384]{1,0:T(8,128)(2,1)} %param.4) | copy-start | bytes 3538948
  0.6 1.9 %copy-start.1 = (bf16[1,128,1536]{2,1,0:T(8,128)(2,1)S(1)}, bf16[1,128,1536]{2,1,0:T(8,128)(2,1)}, u32[]{:S(2)}) copy-start(bf16[1,128,1536]{2,1,0:T(8,128)(2,1)} %param.3) | copy-start | bytes 1179652
  3.7 15.4 %copy-start.11 = (s32[128,6]{0,1:T(8,128)S(1)}, s32[128,6]{0,1:T(8,128)}, u32[]{:S(2)}) copy-start(s32[128,6]{0,1:T(8,128)} %param.5) | copy-start | bytes 9220
  7.6 23.7 %all-to-all-start = ((bf16[128,2,768]{2,1,0:T(2,128)(2,1)}), bf16[128,2,768]{2,1,0:T(2,128)(2,1)S(1)}, u32[]{:S(2)}, u32[]{:S(2)}) async-start(bf16[128,2,768]{2,1,0:T(2,128)(2,1)} %reshape.131), calls=%async_computation | async-start | bytes 786432 | tf_op jit(solution)/shard_map/all_to_all | solution.py:42
  40.1 46.9 %all-to-all-start.1 = ((bf16[6,128,1,1536]{3,0,2,1:T(8,128)(2,1)}), bf16[6,128,1,1536]{3,0,2,1:T(8,128)(2,1)}, u32[]{:S(2)}, u32[]{:S(2)}) async-start(bf16[6,128,1,1536]{3,0,2,1:T(8,128)(2,1)} %copy.16), calls=%async_computation.1 | async-start | bytes 6291456 | tf_op jit(solution)/shard_map/all_to_all | solution.py:54
  46.3 1.7 %copy-start.4 = (f32[128,384]{1,0:T(8,128)}, f32[128,384]{1,0:T(8,128)S(1)}, u32[]{:S(2)}) copy-start(f32[128,384]{1,0:T(8,128)S(1)} %get-tuple-element.5) | copy-start | bytes 589828
  94.3 1.5 copy-start.8
  95.8 6.0 %copy-start.10 = (f32[128,128]{1,0:T(8,128)S(1)}, f32[128,128]{1,0:T(8,128)}, u32[]{:S(2)}) copy-start(f32[128,128]{1,0:T(8,128)} %fusion.31) | copy-start | bytes 196612
  97.1 21.2 %all-to-all-start.2 = ((bf16[6,128,1,384]{3,0,2,1:T(8,128)(2,1)}), bf16[6,128,1,384]{3,0,2,1:T(8,128)(2,1)S(1)}, u32[]{:S(2)}, u32[]{:S(2)}) async-start(bf16[6,128,1,384]{3,0,2,1:T(8,128)(2,1)} %copy.19), calls=%async_computation.2 | async-start | bytes 1572864 | tf_op jit(solution)/shard_map/all_to_all | solution.py:75
  104.9 19.8 %copy-start.7 = (f32[128,384]{1,0:T(8,128)S(1)}, f32[128,384]{1,0:T(8,128)}, u32[]{:S(2)}) copy-start(f32[128,384]{1,0:T(8,128)} %fusion.67) | copy-start | bytes 589828
  104.9 19.8 %copy-start.9 = (f32[128,384]{1,0:T(8,128)S(1)}, f32[128,384]{1,0:T(8,128)}, u32[]{:S(2)}) copy-start(f32[128,384]{1,0:T(8,128)} %convolution_bitcast_fusion.1) | copy-start | bytes 589828
  120.0 14.6 %all-to-all-start.3 = ((bf16[128,2,192]{2,1,0:T(2,128)(2,1)}), bf16[128,2,192]{2,1,0:T(2,128)(2,1)S(1)}, u32[]{:S(2)}, u32[]{:S(2)}) async-start(bf16[128,2,192]{2,1,0:T(2,128)(2,1)} %reshape.133), calls=%async_computation.3 | async-start | bytes 262144 | tf_op jit(solution)/shard_map/all_to_all | solution.py:83
  125.0 12.0 %copy-start.2 = (f32[128,384]{1,0:T(8,128)}, f32[128,384]{1,0:T(8,128)S(1)}, u32[]{:S(2)}) copy-start(f32[128,384]{1,0:T(8,128)S(1)} %get-tuple-element.7) | copy-start | bytes 589828
  138.3 4.5 %copy-start.3 = (f32[128,384]{1,0:T(8,128)S(1)}, f32[128,384]{1,0:T(8,128)}, u32[]{:S(2)}) copy-start(f32[128,384]{1,0:T(8,128)} %copy-done.2) | copy-start | bytes 589828
  138.3 4.5 %copy-start.5 = (f32[128,384]{1,0:T(8,128)S(1)}, f32[128,384]{1,0:T(8,128)}, u32[]{:S(2)}) copy-start(f32[128,384]{1,0:T(8,128)} %copy-done.4) | copy-start | bytes 589828
  138.3 4.5 %copy-start.6 = (bf16[128,1,384]{2,1,0:T(2,128)(2,1)S(1)}, bf16[128,1,384]{2,1,0:T(2,128)(2,1)}, u32[]{:S(2)}) copy-start(bf16[128,1,384]{2,1,0:T(2,128)(2,1)} %reshape.134) | copy-start | bytes 294916
  138.3 29.3 %all-to-all-start.4 = ((bf16[128,12,384]{2,1,0:T(8,128)(2,1)}), bf16[128,12,384]{2,1,0:T(8,128)(2,1)S(1)}, u32[]{:S(2)}, u32[]{:S(2)}) async-start(bf16[128,12,384]{2,1,0:T(8,128)(2,1)} %reshape.108), calls=%async_computation.4 | async-start | bytes 3145728 | tf_op jit(solution)/shard_map/all_to_all | solution.py:88

commit v2 on v1

--- a/solution.py
+++ b/solution.py
@@ -1,6 +1,10 @@
+import functools
+
 import jax
 import jax.numpy as jnp
 from jax import lax
+from jax.experimental import pallas as pl
+from jax.experimental.pallas import tpu as pltpu
 from jax.sharding import PartitionSpec as P
 
 EPS = 1e-06
@@ -9,11 +13,141 @@
 WEIGHT_SELF = 0.1
 SHIFT_PAIR = 0.12
 WEIGHT_PAIR = 0.5
-
-
-def unit_rows(features):
-    values = features.astype(jnp.float32)
-    return values * lax.rsqrt(jnp.sum(values * values, axis=-1, keepdims=True) + EPS)
+MESH = pl.DeviceIdType.MESH
+SIDE = 4
+RING = 32
+KNN = 6
+
+
+def place(orient, index):
+    y, x, z, c = index >> 5, (index >> 3) & 3, (index >> 1) & 3, index & 1
+    if orient == 0:
+        return y, index & 31
+    if orient == 1:
+        return x, (y << 3) + (index & 7)
+    return z, ((index >> 3) << 1) + c
+
+
+def device_at(orient, layer, spot):
+    if orient == 0:
+        return (layer << 5) + spot
+    if orient == 1:
+        return ((spot >> 3) << 5) + (layer << 3) + (spot & 7)
+    return ((spot >> 1) << 3) + (layer << 1) + (spot & 1)
+
+
+def shifted(spot, step):
+    a = ((spot >> 3) + (step >> 3)) & 3
+    b = ((spot >> 1) + (step >> 1)) & 3
+    return (a << 3) + (b << 1) + ((spot + step) & 1)
+
+
+def remote(src, dst, send, recv, device):
+    return pltpu.make_async_remote_copy(
+        src_ref=src, dst_ref=dst, send_sem=send, recv_sem=recv, device_id=(device,), device_id_type=MESH
+    )
+
+
+def front(nb_ref, teacher_ref, unit_ref, partner_ref, held0, held1, held2, picked, own_sem, send1, recv1, send2, recv2, send3, recv3):
+    held = (held0, held1, held2)
+    me = lax.axis_index("dp")
+    where = [place(o, me) for o in range(3)]
+    barrier = pltpu.get_barrier_semaphore()
+
+    def greet(step, carry):
+        for o in range(3):
+            layer, spot = where[o]
+            pl.semaphore_signal(barrier, inc=1, device_id=(device_at(o, layer, shifted(spot, step)),), device_id_type=MESH)
+        return carry
+
+    lax.fori_loop(1, RING, greet, 0)
+    values = teacher_ref[0].astype(jnp.float32)
+    total = jnp.sum(values * values, axis=-1, keepdims=True)
+    unit_ref[...] = (values * lax.rsqrt(total + EPS)).astype(jnp.bfloat16)
+    pl.semaphore_wait(barrier, 3 * (RING - 1))
+
+    def tile(ref, o, spot):
+        rows = pl.ds(pl.multiple_of((spot >> 2) * 16, 16), 16)
+        cols = pl.ds(pl.multiple_of(512 * o + (spot & 3) * 128, 128), 128)
+        return ref.at[rows, cols]
+
+    def deal(step, carry):
+        for o in range(3):
+            layer, spot = where[o]
+            target = shifted(spot, step)
+            remote(
+                tile(unit_ref, o, target), held[o].at[layer * RING + spot], send1.at[o], recv1.at[o],
+                device_at(o, layer, target),
+            ).start()
+        return carry
+
+    own = []
+    for o in range(3):
+        layer, spot = where[o]
+        own.append(pltpu.make_async_copy(tile(unit_ref, o, spot), held[o].at[layer * RING + spot], own_sem.at[o]))
+        own[o].start()
+    lax.fori_loop(1, RING, deal, 0)
+    for o in range(3):
+        layer, spot = where[o]
+        own[o].wait()
+        part = held[o].at[pl.ds(0, RING - 1)]
+        remote(part, part, send1.at[o], recv1.at[o], me).wait()
+        mine = held[o].at[pl.ds(layer * RING, RING)]
+        for hop in range(1, SIDE):
+            remote(mine, mine, send2.at[o], recv2.at[o], device_at(o, (layer + hop) & 3, spot)).start()
+
+    for o in range(3):
+        layer, spot = where[o]
+        part = held[o].at[pl.ds(0, RING * (SIDE - 1))]
+        remote(part, part, send2.at[o], recv2.at[o], me).wait()
+    rows_of = [(pl.ds(pl.multiple_of((where[o][1] >> 2) * 16, 16), 16),
+                pl.ds(pl.multiple_of(512 * o + (where[o][1] & 3) * 128, 128), 128)) for o in range(3)]
+
+    def pick(o, step):
+        layer, spot = where[o]
+        asker = device_at(o, layer, shifted(spot, step))
+        for k in range(KNN):
+            up, at = place(o, nb_ref[k, asker])
+            picked[o, step, k] = held[o][(up << 5) + at]
+        return asker
+
+    for o in range(3):
+        pick(o, 0)
+        pltpu.make_async_copy(picked.at[o, 0], partner_ref.at[:, rows_of[o][0], rows_of[o][1]], own_sem.at[o]).start()
+
+    def serve(step, carry):
+        for o in range(3):
+            asker = pick(o, step)
+            remote(
+                picked.at[o, step], partner_ref.at[:, rows_of[o][0], rows_of[o][1]], send3.at[o], recv3.at[o], asker
+            ).start()
+        return carry
+
+    lax.fori_loop(1, RING, serve, 0)
+    for o in range(3):
+        pltpu.make_async_copy(picked.at[o, 0], picked.at[o, 0], own_sem.at[o]).wait()
+        part = picked.at[o, pl.ds(1, RING - 1)]
+        remote(part, part, send3.at[o], recv3.at[o], me).wait()
+
+
+def fetch(teacher, neighbours):
+    smem = pl.BlockSpec(memory_space=pltpu.SMEM)
+    vmem = pl.BlockSpec(memory_space=pltpu.VMEM)
+    return pl.pallas_call(
+        front,
+        out_shape=(
+            jax.ShapeDtypeStruct((128, 1536), jnp.bfloat16),
+            jax.ShapeDtypeStruct((KNN, 128, 1536), jnp.bfloat16),
+        ),
+        in_specs=[smem, vmem],
+        out_specs=(vmem, vmem),
+        scratch_shapes=[pltpu.VMEM((128, 16, 128), jnp.bfloat16)] * 3
+        + [pltpu.VMEM((3, RING, KNN, 16, 128), jnp.bfloat16)]
+        + [pltpu.SemaphoreType.DMA((3,))] * 7,
+        compiler_params=pltpu.CompilerParams(
+            collective_id=0, has_side_effects=True, vmem_limit_bytes=32 * 2**20
+        ),
+    )(jnp.transpose(neighbours), teacher)
 
 
 def code_scale(codes):
@@ -34,14 +168,11 @@
     rows = patches // count
     images = neighbours.shape[0]
     slots = neighbours.shape[1]
-    own_unit = unit_rows(teacher[0]).astype(jnp.bfloat16)
+    own_unit, partner_units = fetch(teacher, neighbours)
     codes = jnp.dot(own_unit, head_weight, preferred_element_type=jnp.float32).astype(jnp.bfloat16)
     own_inv = code_scale(codes)
     own_code = (codes.astype(jnp.float32) * own_inv).astype(jnp.bfloat16)
-    unit_pieces = own_unit.reshape(count, rows, width)
-    held_units = lax.all_to_all(unit_pieces, "dp", split_axis=0, concat_axis=0, tiled=True)
     order = jnp.transpose(neighbours)
-    send_units = held_units[order]
     tcorr_self = jnp.einsum("pd,qd->pq", own_unit, own_unit, preferred_element_type=jnp.float32)
     scor_self = jnp.einsum("pc,qc->pq", own_code, own_code, preferred_element_type=jnp.float32)
     gate_self = (
@@ -51,16 +182,13 @@
     grad_self = grad_self + jnp.einsum(
         "qp,qc->pc", gate_self, own_code, preferred_element_type=jnp.float32
     )
-    partner_units = lax.all_to_all(send_units, "dp", split_axis=1, concat_axis=1, tiled=True)
-    items = partner_units.shape[0]
-    finish_partner_units = partner_units.reshape(items, patches, width)
     finish_partner_codes = jnp.einsum(
-        "nqd,dc->nqc", finish_partner_units, head_weight, preferred_element_type=jnp.float32
+        "nqd,dc->nqc", partner_units, head_weight, preferred_element_type=jnp.float32
     ).astype(jnp.bfloat16)
     partner_inv = code_scale(finish_partner_codes)
     partner_code = (finish_partner_codes.astype(jnp.float32) * partner_inv).astype(jnp.bfloat16)
     tcorr = jnp.einsum(
-        "pd,nqd->npq", own_unit, finish_partner_units, preferred_element_type=jnp.float32
+        "pd,nqd->npq", own_unit, partner_units, preferred_element_type=jnp.float32
     )
     scor = jnp.einsum("pc,nqc->npq", own_code, partner_code, preferred_element_type=jnp.float32)
     gate = (-(LOSS_SCALE * WEIGHT_PAIR) * (tcorr - SHIFT_PAIR) * jnp.maximum(scor, 0.0)).astype(
@@ -69,7 +197,6 @@
     grads = jnp.einsum("npq,nqc->npc", gate, partner_code, preferred_element_type=jnp.float32)
     cross_raw = jnp.einsum("npq,pc->nqc", gate, own_code, preferred_element_type=jnp.float32)
     cross = back_norm(cross_raw, partner_code, partner_inv).astype(jnp.bfloat16)
-    grads, cross = (grads, cross)
     grad_total = grad_self + jnp.sum(grads, axis=0)
     own_grad = back_norm(grad_total, own_code, own_inv)
     arrived = lax.all_to_all(

time: 169 us -> 128 us (0.76)
  waiting for transfers between devices: 98.3 us -> 47.4 us
  Pallas kernels: 0 us -> 46.3 us
  starting transfers between devices: 31 us -> 16.8 us
  local copies, waits for them, and re-layouts: 14.4 us -> 5.8 us
  matrix products: 15.2 us -> 7.38 us
  other arithmetic: 8.71 us -> 3.41 us
    all_to_all x2 -> x0, waiting for transfers between devices: 51.2 us -> none  [the longest x1 39.1 us: body(): lax.all_to_all(send_units, 'dp', split_axis=1, concat_axis=1, tiled=True)]
    pallas_call x0 -> x1, Pallas kernels: none -> 46.3 us  [fetch(): pl.pallas_call(front, out_shape=(jax.ShapeDtypeStruct((128, 1536), jnp.bf...]
    all_to_all x2 -> x0, starting transfers between devices: 17.2 us -> none  [the longest x1 11.5 us: body(): lax.all_to_all(unit_pieces, 'dp', split_axis=0, concat_axis=0, tiled=True)]
    gather x2 -> x0, local copies, waits for them, and re-layouts: 8.44 us -> none  [body(): send_units = held_units[order]]
    convert_element_type x4 -> x0, other arithmetic: 6.08 us -> none  [the longest x3 4.36 us: body(): own_unit = unit_rows(teacher[0]).astype(jnp.bfloat16)]
    dot_general x2, matrix products: 6.84 us -> 2.25 us  [the longest x1 1.47 us: body(): jnp.einsum('nqd,dc->nqc', partner_units, head_weight, preferred_element_t...]
    all_to_all x1, starting transfers between devices: 4.73 us -> 7.83 us  [body(): lax.all_to_all(cross.reshape(slots, count, rows, code_width), 'dp', split...]
  transfers between devices with their start and end apart: 5 -> 3, of which waited for: 5 -> 3; matrix products, arithmetic and copies ran while one was open for 4% -> 3% of each run, Pallas kernels for 0% -> 0%
where the time goes in v2:
time: 128 us
  waiting for transfers between devices  47.4 us (37%)
  Pallas kernels  46.3 us (36%)
  starting transfers between devices  16.8 us (13%)
  matrix products  7.38 us (6%)
  local copies, waits for them, and re-layouts  5.8 us (5%)
  other arithmetic  3.41 us (3%)
    pallas_call x1, Pallas kernels, fetch(): pl.pallas_call(front, out_shape=(jax.ShapeDtypeStruct((128, 1536), jnp.bf...  46.3 us
    all_to_all x1, waiting for transfers between devices, body(): lax.all_to_all(shares, 'dp', split_axis=0, concat_axis=0, tiled=True)  23.1 us
    all_to_all x1, waiting for transfers between devices, body(): lax.all_to_all(cross.reshape(slots, count, rows, code_width), 'dp', split...  14.6 us
    all_to_all x1, waiting for transfers between devices, body(): lax.all_to_all(relayed, 'dp', split_axis=0, concat_axis=0, tiled=True)  9.66 us
    all_to_all x1, starting transfers between devices, body(): lax.all_to_all(cross.reshape(slots, count, rows, code_width), 'dp', split...  7.83 us
    all_to_all x1, starting transfers between devices, body(): lax.all_to_all(relayed, 'dp', split_axis=0, concat_axis=0, tiled=True)  4.63 us
    all_to_all x1, starting transfers between devices, body(): lax.all_to_all(shares, 'dp', split_axis=0, concat_axis=0, tiled=True)  4.31 us
    unnamed x14, local copies, waits for them, and re-layouts  2.74 us
  transfers between devices with their start and end apart: 3, of which 3 were waited for; matrix products, arithmetic and copies ran while one was open for 3% of the time, Pallas kernels for 0%

profile of v2, /device:TPU:1, one launch (start us, length us, event | category | flops | bytes accessed | tf_op | source)
XLA Modules:
  0.0 127.9 jit_solution(17086333228696981513)
XLA Ops:
  0.6 0.0 copy-start
  0.6 0.0 copy-start.1
  0.7 1.1 copy-done.1
  1.7 0.0 copy-start.2
  1.7 0.7 copy-done.2
  2.4 46.3 %shard_map.50 = (bf16[128,1536]{1,0:T(8,128)(2,1)S(1)}, bf16[6,128,1536]{2,1,0:T(8,128)(2,1)S(1)}) custom-call(s32[6,128]{1,0:T(8,128)S(1)} %bitcast.63, bf16[1,128,1536]{2,1,0:T(8,128)(2,1)S(1)} %copy-done.1), custom_call_target="tpu_custom_call" | custom-call | tf_op jit(solution)/shard_map/pallas_call | solution.py:136
  48.8 0.0 copy-done
  48.8 0.5 multiply_reduce_fusion
  49.2 1.5 %fusion.7 = (f32[6,128]{1,0:T(8,128)S(1)}, bf16[6,128,384]{2,1,0:T(8,128)(2,1)S(1)}) fusion(bf16[6,128,1536]{2,1,0:T(8,128)(2,1)S(1)} %get-tuple-element.5, bf16[1536,384]{1,0:T(8,128)(2,1)S(1)} %copy-done), kind=kOutput, calls=%fused_computation.16 | convolution fusion | flops 907148544 | bytes 4131840 | tf_op jit(solution)/shard_map/nqd,dc->nqc/dot_general | solution.py:185
  50.7 0.1 multiply_convert_fusion
  50.8 0.4 convolution_maximum_fusion
  51.2 0.8 fusion.12
  52.0 1.5 %fusion.4 = bf16[6,128,1,384]{3,1,0,2:T(8,128)(2,1)S(1)} fusion(f32[6,128]{1,0:T(8,128)S(1)} %add_rsqrt_fusion, bf16[6,128,384]{2,1,0:T(8,128)(2,1)S(1)} %get-tuple-element.7, bf16[6,128,128]{1,2,0:T(8,128)(2,1)S(1)} %fusion.12, bf16[128,384]{1,0:T(8,128)(2,1)S(1)} %multiply_convert_fusion), kind=kOutput, calls=%fused_computation.11 | convolution fusion | flops 154829952 | bytes 1477632 | tf_op jit(solution)/shard_map/mul | solution.py:160
  53.5 1.2 copy.8
  54.7 7.8 %all-to-all-start = ((bf16[6,128,1,384]{3,0,2,1:T(8,128)(2,1)}), bf16[6,128,1,384]{3,0,2,1:T(8,128)(2,1)S(1)}, u32[]{:S(2)}, u32[]{:S(2)}) async-start(bf16[6,128,1,384]{3,0,2,1:T(8,128)(2,1)} %copy.8), calls=%async_computation | async-start | bytes 1572864 | tf_op jit(solution)/shard_map/all_to_all | solution.py:202
  62.6 0.0 copy-start.3
  62.6 0.3 fusion.17
  62.9 1.1 convolution_bitcast_fusion.1
  63.9 0.0 copy-start.5
  63.9 0.2 fusion.18
  64.1 0.2 fusion.44
  64.3 14.6 %all-to-all-done = bf16[6,128,1,384]{3,0,2,1:T(8,128)(2,1)S(1)} async-done(((bf16[6,128,1,384]{3,0,2,1:T(8,128)(2,1)}), bf16[6,128,1,384]{3,0,2,1:T(8,128)(2,1)S(1)}, u32[]{:S(2)}, u32[]{:S(2)}) %all-to-all-start) | async-done | bytes 589856 | tf_op jit(solution)/shard_map/all_to_all | solution.py:202
  78.9 0.0 copy-done.3
  78.9 0.3 fusion.15
  79.2 0.5 broadcast.29
  79.7 0.7 reduce
  80.4 0.8 reshape.42
  81.2 4.6 %all-to-all-start.1 = ((bf16[128,2,192]{2,1,0:T(2,128)(2,1)}), bf16[128,2,192]{2,1,0:T(2,128)(2,1)S(1)}, u32[]{:S(2)}, u32[]{:S(2)}) async-start(bf16[128,2,192]{2,1,0:T(2,128)(2,1)} %reshape.42), calls=%async_computation.1 | async-start | bytes 262144 | tf_op jit(solution)/shard_map/all_to_all | solution.py:210
  85.8 0.0 copy-done.5
  85.8 0.3 fusion.26
  86.1 9.7 %all-to-all-done.1 = bf16[128,2,192]{2,1,0:T(2,128)(2,1)S(1)} async-done(((bf16[128,2,192]{2,1,0:T(2,128)(2,1)}), bf16[128,2,192]{2,1,0:T(2,128)(2,1)S(1)}, u32[]{:S(2)}, u32[]{:S(2)}) %all-to-all-start.1) | async-done | bytes 98336 | tf_op jit(solution)/shard_map/all_to_all | solution.py:210
  95.8 0.2 reshape.43
  95.9 0.0 copy-start.4
  95.9 0.6 convolution_convert_fusion
  96.5 1.3 %reshape.35 = bf16[128,12,384]{2,1,0:T(8,128)(2,1)} reshape(bf16[1536,384]{1,0:T(8,128)(2,1)S(1)} %convolution_convert_fusion) | data formatting | bytes 2359296 | tf_op jit(solution)/shard_map/reshape | solution.py:214
  97.8 0.0 copy-done.4
  97.8 4.3 %all-to-all-start.2 = ((bf16[128,12,384]{2,1,0:T(8,128)(2,1)}), bf16[128,12,384]{2,1,0:T(8,128)(2,1)S(1)}, u32[]{:S(2)}, u32[]{:S(2)}) async-start(bf16[128,12,384]{2,1,0:T(8,128)(2,1)} %reshape.35), calls=%async_computation.2 | async-start | bytes 3145728 | tf_op jit(solution)/shard_map/all_to_all | solution.py:215
  102.1 1.7 %fusion.42 = f32[1,128,384]{2,1,0:T(8,128)} fusion(bf16[128,1,384]{2,1,0:T(2,128)(2,1)} %copy-done.4, f32[128]{0:T(128)S(1)} %add_rsqrt_fusion.1, f32[128,384]{1,0:T(8,128)S(1)} %get-tuple-element.11, f32[128]{0:T(128)S(1)} %get-tuple-element.10, f32[128,384]{1,0:T(8,128)S(1)} %get-tuple-element.9), kind=kLoop, calls=%fused_computation.56 | loop fusion | flops 393216 | bytes 689152 | tf_op jit(solution)/shard_map/broadcast_in_dim | solution.py:217
  103.9 23.1 %all-to-all-done.2 = bf16[128,12,384]{2,1,0:T(8,128)(2,1)S(1)} async-done(((bf16[128,12,384]{2,1,0:T(8,128)(2,1)}), bf16[128,12,384]{2,1,0:T(8,128)(2,1)S(1)}, u32[]{:S(2)}, u32[]{:S(2)}) %all-to-all-start.2) | async-done | bytes 1179680 | tf_op jit(solution)/shard_map/all_to_all | solution.py:215
  127.0 0.9 convert_reduce_fusion
  (2 shorter events, 0.0 us)
Async XLA Ops:
  0.6 48.1 %copy-start = (bf16[1536,384]{1,0:T(8,128)(2,1)S(1)}, bf16[1536,384]{1,0:T(8,128)(2,1)}, u32[]{:S(2)}) copy-start(bf16[1536,384]{1,0:T(8,128)(2,1)} %param.4) | copy-start | bytes 3538948
  0.6 1.1 copy-start.1
  1.7 0.7 copy-start.2
  54.7 24.2 %all-to-all-start = ((bf16[6,128,1,384]{3,0,2,1:T(8,128)(2,1)}), bf16[6,128,1,384]{3,0,2,1:T(8,128)(2,1)S(1)}, u32[]{:S(2)}, u32[]{:S(2)}) async-start(bf16[6,128,1,384]{3,0,2,1:T(8,128)(2,1)} %copy.8), calls=%async_computation | async-start | bytes 1572864 | tf_op jit(solution)/shard_map/all_to_all | solution.py:202
  62.6 16.3 %copy-start.3 = (s32[128,6]{0,1:T(8,128)S(1)}, s32[128,6]{0,1:T(8,128)}, u32[]{:S(2)}) copy-start(s32[128,6]{0,1:T(8,128)} %param.5) | copy-start | bytes 9220
  63.9 21.9 %copy-start.5 = (f32[128,384]{1,0:T(8,128)S(1)}, f32[128,384]{1,0:T(8,128)}, u32[]{:S(2)}) copy-start(f32[128,384]{1,0:T(8,128)} %convolution_bitcast_fusion.1) | copy-start | bytes 589828
  81.2 14.6 %all-to-all-start.1 = ((bf16[128,2,192]{2,1,0:T(2,128)(2,1)}), bf16[128,2,192]{2,1,0:T(2,128)(2,1)S(1)}, u32[]{:S(2)}, u32[]{:S(2)}) async-start(bf16[128,2,192]{2,1,0:T(2,128)(2,1)} %reshape.42), calls=%async_computation.1 | async-start | bytes 262144 | tf_op jit(solution)/shard_map/all_to_all | solution.py:210
  95.9 1.9 %copy-start.4 = (bf16[128,1,384]{2,1,0:T(2,128)(2,1)}, bf16[128,1,384]{2,1,0:T(2,128)(2,1)S(1)}, u32[]{:S(2)}) copy-start(bf16[128,1,384]{2,1,0:T(2,128)(2,1)S(1)} %reshape.43) | copy-start | bytes 294916
  97.8 29.1 %all-to-all-start.2 = ((bf16[128,12,384]{2,1,0:T(8,128)(2,1)}), bf16[128,12,384]{2,1,0:T(8,128)(2,1)S(1)}, u32[]{:S(2)}, u32[]{:S(2)}) async-start(bf16[128,12,384]{2,1,0:T(8,128)(2,1)} %reshape.35), calls=%async_computation.2 | async-start | bytes 3145728 | tf_op jit(solution)/shard_map/all_to_all | solution.py:215

commit v3 on v2

v3 whole, which is shorter than its diff:
```python
import jax
import jax.numpy as jnp
from jax import lax
from jax.experimental import pallas as pl
from jax.experimental.pallas import tpu as pltpu
from jax.sharding import PartitionSpec as P

EPS = 1e-06
LOSS_SCALE = 128.0
SHIFT_SELF = 0.18
WEIGHT_SELF = 0.1
SHIFT_PAIR = 0.12
WEIGHT_PAIR = 0.5
MESH = pl.DeviceIdType.MESH
SIDE = 4
RING = 32
KNN = 6


def place(orient, index):
    y, x, z, c = index >> 5, (index >> 3) & 3, (index >> 1) & 3, index & 1
    if orient == 0:
        return y, index & 31
    if orient == 1:
        return x, (y << 3) + (index & 7)
    return z, ((index >> 3) << 1) + c


def device_at(orient, layer, spot):
    if orient == 0:
        return (layer << 5) + spot
    if orient == 1:
        return ((spot >> 3) << 5) + (layer << 3) + (spot & 7)
    return ((spot >> 1) << 3) + (layer << 1) + (spot & 1)


def shifted(spot, step):
    a = ((spot >> 3) + (step >> 3)) & 3
    b = ((spot >> 1) + (step >> 1)) & 3
    return (a << 3) + (b << 1) + ((spot + step) & 1)


def remote(src, dst, send, recv, device):
    return pltpu.make_async_remote_copy(
        src_ref=src, dst_ref=dst, send_sem=send, recv_sem=recv, device_id=(device,), device_id_type=MESH
    )


def unit_rows(values):
    total = jnp.sum(values * values, axis=-1, keepdims=True)
    return (values * lax.rsqrt(total + EPS)).astype(jnp.bfloat16)


def code_rows(codes):
    values = codes.astype(jnp.bfloat16).astype(jnp.float32)
    inverse = lax.rsqrt(jnp.sum(values * values, axis=-1, keepdims=True) + EPS)
    return (values * inverse).astype(jnp.bfloat16), inverse


def back_norm(grad, code_unit, inverse):
    values = code_unit.astype(jnp.float32)
    return (grad - values * jnp.sum(values * grad, axis=-1, keepdims=True)) * inverse


def dot(a, b, dims=((1,), (0,))):
    return lax.dot_general(a, b, (dims, ((), ())), preferred_element_type=jnp.float32)


def step_kernel(
    nb_ref, nbv_ref, teacher_hbm, weight_hbm, head_ref, grad_ref,
    teacher_ref, weight_ref, unit_ref, code_ref, inv_ref, self_ref, tall_ref, tallp_ref, perm_ref, member_ref,
    held0, held1, held2, picked, partner_ref, cross_out, cross_in, back_out, back_mid, back_in,
    share_out, share_mid, share_sum, share_in,
    load_sem, own_sem, send1, recv1, send2, recv2, send3, recv3, send4, recv4,
):
    held = (held0, held1, held2)
    me = lax.axis_index("dp")
    where = [place(o, me) for o in range(3)]
    column, lane = me >> 3, me & 7
    chip, core = me >> 1, me & 1
    barrier = pltpu.get_barrier_semaphore()
    loads = [
        pltpu.make_async_copy(teacher_hbm.at[0], teacher_ref, load_sem.at[0]),
        pltpu.make_async_copy(weight_hbm, weight_ref, load_sem.at[1]),
    ]
    for load in loads:
        load.start()

    def greet(step, carry):
        for o in range(3):
            layer, spot = where[o]
            pl.semaphore_signal(barrier, inc=1, device_id=(device_at(o, layer, shifted(spot, step)),), device_id_type=MESH)
        return carry

    lax.fori_loop(1, RING, greet, 0)
    loads[0].wait()
    unit_ref[...] = unit_rows(teacher_ref[...].astype(jnp.float32))
    pl.semaphore_wait(barrier, 3 * (RING - 1))

    def tile(ref, o, spot):
        rows = pl.ds(pl.multiple_of((spot >> 2) * 16, 16), 16)
        cols = pl.ds(pl.multiple_of(512 * o + (spot & 3) * 128, 128), 128)
        return ref.at[rows, cols]

    def deal(step, carry):
        for o in range(3):
            layer, spot = where[o]
            target = shifted(spot, step)
            remote(
                tile(unit_ref, o, target), held[o].at[layer * RING + spot], send1.at[o], recv1.at[o],
                device_at(o, layer, target),
            ).start()
        return carry

    own = []
    for o in range(3):
        layer, spot = where[o]
        own.append(pltpu.make_async_copy(tile(unit_ref, o, spot), held[o].at[layer * RING + spot], own_sem.at[o]))
        own[o].start()
    lax.fori_loop(1, RING, deal, 0)

    loads[1].wait()
    code_unit, inverse = code_rows(dot(unit_ref[...], weight_ref[...]))
    code_ref[...] = code_unit
    inv_ref[...] = jnp.broadcast_to(inverse, inv_ref.shape)

    for o in range(3):
        layer, spot = where[o]
        own[o].wait()
        part = held[o].at[pl.ds(0, RING - 1)]
        remote(part, part, send1.at[o], recv1.at[o], me).wait()
        mine = held[o].at[pl.ds(layer * RING, RING)]
        for hop in range(1, SIDE):
            remote(mine, mine, send2.at[o], recv2.at[o], device_at(o, (layer + hop) & 3, spot)).start()

    units, codes = unit_ref[...], code_ref[...]
    tcorr = dot(units, units, ((1,), (1,)))
    scor = dot(codes, codes, ((1,), (1,)))
    gate = (-(LOSS_SCALE * WEIGHT_SELF) * (tcorr - SHIFT_SELF) * jnp.maximum(scor, 0.0)).astype(jnp.bfloat16)
    self_ref[...] = dot(gate, codes) + dot(gate, codes, ((0,), (0,)))

    for o in range(3):
        part = held[o].at[pl.ds(0, RING * (SIDE - 1))]
        remote(part, part, send2.at[o], recv2.at[o], me).wait()
    spans = [(pl.ds(pl.multiple_of((where[o][1] >> 2) * 16, 16), 16),
              pl.ds(pl.multiple_of(512 * o + (where[o][1] & 3) * 128, 128), 128)) for o in range(3)]

    def pick(o, step):
        layer, spot = where[o]
        asker = device_at(o, layer, shifted(spot, step))
        for k in range(KNN):
            up, at = place(o, nb_ref[k, asker])
            picked[o, step, k] = held[o][(up << 5) + at]
        return asker

    for o in range(3):
        pick(o, 0)
        pltpu.make_async_copy(picked.at[o, 0], partner_ref.at[:, spans[o][0], spans[o][1]], own_sem.at[o]).start()

    def serve(step, carry):
        for o in range(3):
            asker = pick(o, step)
            remote(
                picked.at[o, step], partner_ref.at[:, spans[o][0], spans[o][1]], send3.at[o], recv3.at[o], asker
            ).start()
        return carry

    lax.fori_loop(1, RING, serve, 0)

    row = lax.broadcasted_iota(jnp.int32, (1024, 768), 0)
    col = lax.broadcasted_iota(jnp.int32, (1024, 768), 1)
    perm_ref[...] = jnp.where(col == ((row & 7) << 7) + (row >> 3), 1.0, 0.0).astype(jnp.bfloat16)
    image = lax.broadcasted_iota(jnp.int32, (128, 128), 0)
    member = jnp.concatenate(
        [jnp.where(image == nbv_ref[k : k + 1, :], 1.0, 0.0).astype(jnp.bfloat16) for k in range(KNN)], axis=1
    )
    member_ref[...] = dot(member, perm_ref[...], ((1,), (1,))).astype(jnp.bfloat16)
    tall_ref[...] = jnp.transpose(unit_ref[...].astype(jnp.float32))
    tallp_ref[...] = jnp.zeros_like(tallp_ref)

    def spread(pair, carry):
        both = tall_ref[pl.ds(pl.multiple_of(pair * 24, 8), 24), :]
        tallp_ref[2 * pair, 0:12, :] = both[0:12]
        tallp_ref[2 * pair + 1, 0:12, :] = both[12:24]
        return carry

    lax.fori_loop(0, 64, spread, 0)

    for o in range(3):
        pltpu.make_async_copy(picked.at[o, 0], picked.at[o, 0], own_sem.at[o]).wait()
        part = picked.at[o, pl.ds(1, RING - 1)]
        remote(part, part, send3.at[o], recv3.at[o], me).wait()

    partners = partner_ref[...].reshape(KNN * 128, 1536)
    partner_code, partner_inv = code_rows(dot(partners, weight_ref[...]))
    tcorr = dot(partners, unit_ref[...], ((1,), (1,)))
    scor = dot(partner_code, code_ref[...], ((1,), (1,)))
    gate = (-(LOSS_SCALE * WEIGHT_PAIR) * (tcorr - SHIFT_PAIR) * jnp.maximum(scor, 0.0)).astype(jnp.bfloat16)
    cross = back_norm(dot(gate, code_ref[...]), partner_code, partner_inv).astype(jnp.bfloat16)
    cross_out[...] = dot(perm_ref[...], cross).reshape(128, 8, 384).astype(jnp.bfloat16)

    def give(step, carry):
        target = (((column + (step >> 3)) & 3) | ((((column >> 2) + (step >> 5)) & 3) << 2)) << 3
        target = target + (((lane >> 1) + (step >> 1)) & 3) * 2 + ((lane + step) & 1)
        remote(cross_out.at[target], cross_in.at[me], send4.at[0], recv4.at[0], target).start()
        return carry

    lax.fori_loop(1, 128, give, 0)
    cross_in[me] = cross_out[me]
    grad = self_ref[...] + dot(gate, partner_code, ((0,), (0,)))
    self_ref[...] = back_norm(grad, code_ref[...], inv_ref[:, 0:1])
    part = cross_in.at[pl.ds(0, 127)]
    remote(part, part, send4.at[0], recv4.at[0], me).wait()

    piece = dot(member_ref[...], cross_in[...].reshape(1024, 384))
    back_out[:, :, 0, :] = piece.reshape(16, 8, 384)
    for hop in range(1, 8):
        to = (((lane >> 1) + (hop >> 1)) & 3) * 2 + ((lane + hop) & 1)
        remote(back_out.at[:, to], back_mid.at[:, lane], send4.at[1], recv4.at[1], (column << 3) + to).start()
    back_mid[:, lane] = back_out[:, lane]
    part = back_out.at[:, pl.ds(0, 7)]
    remote(part, part, send4.at[1], recv4.at[1], me).wait()
    for hop in range(1, 16):
        to = (((column >> 2) + (hop >> 2)) & 3) * 4 + ((column + hop) & 3)
        remote(back_mid.at[to], back_in.at[column], send4.at[2], recv4.at[2], (to << 3) + lane).start()
    back_in[column] = back_mid[column]
    part = back_in.at[pl.ds(0, 15)]
    remote(part, part, send4.at[2], recv4.at[2], me).wait()
    relayed = back_in[:, :, 0, :].reshape(128, 384).astype(jnp.bfloat16)
    code_grad = self_ref[...] + relayed.astype(jnp.float32)
    grad_ref[0] = code_grad

    tall = tallp_ref[...].astype(jnp.bfloat16).reshape(2048, 128)
    shares = dot(tall, code_grad.astype(jnp.bfloat16)).reshape(64, 2, 16, 384).astype(jnp.bfloat16)
    share_out[0] = shares[:, 0, 0:12]
    share_out[1] = shares[:, 1, 0:12]
    sibling = remote(share_out.at[1 - core], share_mid, send4.at[3], recv4.at[3], me + 1 - 2 * core)
    sibling.start()
    sibling.wait()
    share_sum[...] = (share_out[core].astype(jnp.float32) + share_mid[...].astype(jnp.float32)).astype(jnp.bfloat16)

    def spend(step, carry):
        to = (((chip >> 4) + (step >> 4)) & 3) * 16 + (((chip >> 2) + (step >> 2)) & 3) * 4 + ((chip + step) & 3)
        remote(share_sum.at[to], share_in.at[chip], send4.at[4], recv4.at[4], to * 2 + core).start()
        return carry

    lax.fori_loop(1, 64, spend, 0)
    share_in[chip] = share_sum[chip]
    part = share_in.at[pl.ds(0, 63)]
    remote(part, part, send4.at[4], recv4.at[4], me).wait()
    head_ref[...] = jnp.sum(share_in[...].astype(jnp.float32), axis=0)


def body(teacher, head_weight, neighbours):
    smem = pl.BlockSpec(memory_space=pltpu.SMEM)
    vmem = pl.BlockSpec(memory_space=pltpu.VMEM)
    hbm = pl.BlockSpec(memory_space=pl.ANY)
    slots = jnp.transpose(neighbours)
    half, full = jnp.bfloat16, jnp.float32
    return pl.pallas_call(
        step_kernel,
        out_shape=(jax.ShapeDtypeStruct((12, 384), full), jax.ShapeDtypeStruct((1, 128, 384), full)),
        in_specs=[smem, vmem, hbm, hbm],
        out_specs=(vmem, vmem),
        scratch_shapes=[
            pltpu.VMEM((128, 1536), half),
            pltpu.VMEM((1536, 384), half),
            pltpu.VMEM((128, 1536), half),
            pltpu.VMEM((128, 384), half),
            pltpu.VMEM((128, 128), full),
            pltpu.VMEM((128, 384), full),
            pltpu.VMEM((1536, 128), full),
            pltpu.VMEM((128, 16, 128), full),
            pltpu.VMEM((1024, 768), half),
            pltpu.VMEM((128, 1024), half),
        ]
        + [pltpu.VMEM((128, 16, 128), half)] * 3
        + [
            pltpu.VMEM((3, RING, KNN, 16, 128), half),
            pltpu.VMEM((KNN, 128, 1536), half),
            pltpu.VMEM((128, 8, 384), half),
            pltpu.VMEM((128, 8, 384), half),
            pltpu.VMEM((16, 8, 1, 384), full),
            pltpu.VMEM((16, 8, 1, 384), full),
            pltpu.VMEM((16, 8, 1, 384), full),
            pltpu.VMEM((2, 64, 12, 384), half),
            pltpu.VMEM((64, 12, 384), half),
            pltpu.VMEM((64, 12, 384), half),
            pltpu.VMEM((64, 12, 384), half),
            pltpu.SemaphoreType.DMA((2,)),
        ]
        + [pltpu.SemaphoreType.DMA((3,))] * 7
        + [pltpu.SemaphoreType.DMA((5,))] * 2,
        compiler_params=pltpu.CompilerParams(
            collective_id=0, has_side_effects=True, vmem_limit_bytes=48 * 2**20
        ),
    )(slots, slots, teacher, head_weight)


def solution(mesh):
    return jax.shard_map(
        body,
        mesh=mesh,
        in_specs=(P("dp", None, None), P(), P()),
        out_specs=(P("dp", None), P("dp", None, None)),
        check_vma=False,
    )
```

time: 128 us -> 97.9 us (0.76)
  waiting for transfers between devices: 47.4 us -> 0 us
  Pallas kernels: 46.3 us -> 92.8 us
  starting transfers between devices: 16.8 us -> 0 us
  matrix products: 7.38 us -> 0 us
  other arithmetic: 3.41 us -> 0 us
  local copies, waits for them, and re-layouts: 5.8 us -> 4.23 us
    all_to_all x3 -> x0, waiting for transfers between devices: 47.4 us -> none  [the longest x1 23.1 us: body(): lax.all_to_all(shares, 'dp', split_axis=0, concat_axis=0, tiled=True)]
    pallas_call x1, Pallas kernels: 46.3 us -> 92.8 us  [body(): pl.pallas_call(step_kernel, out_shape=(jax.ShapeDtypeStruct((12, 384), fu...]
    all_to_all x3 -> x0, starting transfers between devices: 16.8 us -> none  [the longest x1 7.83 us: body(): lax.all_to_all(cross.reshape(slots, count, rows, code_width), 'dp', split...]
    dot_general x11 -> x0, matrix products: 5.86 us -> none  [the longest x1 1.47 us: body(): jnp.einsum('nqd,dc->nqc', partner_units, head_weight, preferred_element_t...]
    reshape x2 -> x0, local copies, waits for them, and re-layouts: 2.54 us -> none  [the longest x1 1.3 us: body(): partial_grad.astype(jnp.bfloat16).reshape(count, width // count, code_width)]
    broadcast_in_dim x1 -> x0, other arithmetic: 1.72 us -> none  [body(): return (head_grad, code_grad[None])]
    mul x1 -> x0, matrix products: 1.52 us -> none  [back_norm(): values * jnp.sum(values * grad, axis=-1, keepdims=True)]
    unnamed x14 -> x8, local copies, waits for them, and re-layouts: 2.74 us -> 4.23 us
  transfers between devices with their start and end apart: 3 -> 0, of which waited for: 3 -> 0; matrix products, arithmetic and copies ran while one was open for 3% -> 0% of each run, Pallas kernels for 0% -> 0%
where the time goes in v3:
time: 97.9 us; the launch traced here: 97.7 us
  Pallas kernels  92.8 us (95%)
  local copies, waits for them, and re-layouts  4.23 us (4%)
    pallas_call x1, Pallas kernels, body(): pl.pallas_call(step_kernel, out_shape=(jax.ShapeDtypeStruct((12, 384), fu...  92.8 us
    unnamed x8, local copies, waits for them, and re-layouts  4.23 us

profile of v3, /device:TPU:1, one launch (start us, length us, event | category | flops | bytes accessed | tf_op | source)
XLA Modules:
  0.0 97.7 jit_solution(3807796281959171424)
XLA Ops:
  0.6 0.0 copy-start
  0.6 1.3 %copy-done = bf16[1536,384]{1,0:T(8,128)(2,1)S(1)} copy-done((bf16[1536,384]{1,0:T(8,128)(2,1)S(1)}, bf16[1536,384]{1,0:T(8,128)(2,1)}, u32[]{:S(2)}) %copy-start) | copy-done | bytes 1179672
  1.9 0.0 copy-start.1
  1.9 1.0 %copy-done.1 = bf16[1,128,1536]{2,1,0:T(8,128)(2,1)S(1)} copy-done((bf16[1,128,1536]{2,1,0:T(8,128)(2,1)S(1)}, bf16[1,128,1536]{2,1,0:T(8,128)(2,1)}, u32[]{:S(2)}) %copy-start.1) | copy-done | bytes 393240
  2.9 0.0 copy-start.2
  2.9 0.7 copy-done.2
  3.6 92.8 %shard_map.50 = (f32[12,384]{1,0:T(8,128)S(1)}, f32[1,128,384]{2,1,0:T(8,128)S(1)}) custom-call(s32[6,128]{1,0:T(8,128)S(1)} %bitcast.1, s32[6,128]{1,0:T(8,128)S(1)} %bitcast.2, bf16[1,128,1536]{2,1,0:T(8,128)(2,1)S(1)} %copy-done.1, bf16[1536,384]{1,0:T(8,128)(2,1)S(1)} %copy-done), custom_call_target="tpu_custom_call" | custom-call | tf_op jit(solution)/shard_map/pallas_call | solution.py:260
  96.4 0.6 copy.7
  97.0 0.7 copy.8
Async XLA Ops:
  0.6 1.3 %copy-start = (bf16[1536,384]{1,0:T(8,128)(2,1)S(1)}, bf16[1536,384]{1,0:T(8,128)(2,1)}, u32[]{:S(2)}) copy-start(bf16[1536,384]{1,0:T(8,128)(2,1)} %weight_hbm.1) | copy-start | bytes 3538948
  1.9 1.0 %copy-start.1 = (bf16[1,128,1536]{2,1,0:T(8,128)(2,1)S(1)}, bf16[1,128,1536]{2,1,0:T(8,128)(2,1)}, u32[]{:S(2)}) copy-start(bf16[1,128,1536]{2,1,0:T(8,128)(2,1)} %teacher_hbm.1) | copy-start | bytes 1179652
  2.9 0.7 copy-start.2

commit v4 on v3

v4 whole, which is shorter than its diff:
```python
import jax
import jax.numpy as jnp
from jax import lax
from jax.experimental import pallas as pl
from jax.experimental.pallas import tpu as pltpu
from jax.sharding import PartitionSpec as P

EPS = 1e-06
LOSS_SCALE = 128.0
SHIFT_SELF = 0.18
WEIGHT_SELF = 0.1
SHIFT_PAIR = 0.12
WEIGHT_PAIR = 0.5
MESH = pl.DeviceIdType.MESH
SIDE = 4
RING = 32
KNN = 6


def place(orient, index):
    y, x, z, c = index >> 5, (index >> 3) & 3, (index >> 1) & 3, index & 1
    if orient == 0:
        return y, index & 31
    if orient == 1:
        return x, (y << 3) + (index & 7)
    return z, ((index >> 3) << 1) + c


def device_at(orient, layer, spot):
    if orient == 0:
        return (layer << 5) + spot
    if orient == 1:
        return ((spot >> 3) << 5) + (layer << 3) + (spot & 7)
    return ((spot >> 1) << 3) + (layer << 1) + (spot & 1)


def shifted(spot, step):
    a = ((spot >> 3) + (step >> 3)) & 3
    b = ((spot >> 1) + (step >> 1)) & 3
    return (a << 3) + (b << 1) + ((spot + step) & 1)


def remote(src, dst, send, recv, device):
    return pltpu.make_async_remote_copy(
        src_ref=src, dst_ref=dst, send_sem=send, recv_sem=recv, device_id=(device,), device_id_type=MESH
    )


def unit_rows(values):
    total = jnp.sum(values * values, axis=-1, keepdims=True)
    return (values * lax.rsqrt(total + EPS)).astype(jnp.bfloat16)


def code_rows(codes):
    values = codes.astype(jnp.bfloat16).astype(jnp.float32)
    inverse = lax.rsqrt(jnp.sum(values * values, axis=-1, keepdims=True) + EPS)
    return (values * inverse).astype(jnp.bfloat16), inverse


def back_norm(grad, code_unit, inverse):
    values = code_unit.astype(jnp.float32)
    return (grad - values * jnp.sum(values * grad, axis=-1, keepdims=True)) * inverse


def dot(a, b, dims=((1,), (0,))):
    return lax.dot_general(a, b, (dims, ((), ())), preferred_element_type=jnp.float32)


def digit_sum(place_sum, step):
    return ((((place_sum >> 2) + (step >> 2)) & 3) << 2) + ((place_sum + step) & 3)


SPLIT = ((1, 16), (4, 4), (16, 1))
GREETED = [(0, step) for step in range(1, 32)] + [(1, step) for step in range(8, 32)]
GREETED += [(2, step) for step in range(8, 32) if (step >> 1) & 3]
GREETED.sort(key=lambda at: -(min(at[1] >> 3, 4 - (at[1] >> 3)) + min((at[1] >> 1) & 3, 4 - ((at[1] >> 1) & 3))))


def step_kernel(
    nb_hbm, teacher_hbm, weight_hbm, head_ref, grad_hbm,
    nb_ref, nbv_ref, teacher_ref, weight_ref, unit_ref, both_ref, code_ref, tcode_ref, inv_ref, self_ref, grad_ref,
    perm_ref, pad_ref, member_ref, held0, held1, held2, picked, wide_ref, product_ref, share_ref,
    cross_out, cross_in, part_out, part_in, back_out, back_in,
    out0, out1, out2, mid0, mid1, mid2, sum0, sum1, sum2, in0, in1, in2, plane_out, plane_in,
    load_sem, own_sem, *sems,
):
    held, share_out, share_mid = (held0, held1, held2), (out0, out1, out2), (mid0, mid1, mid2)
    share_sum, layer_in = (sum0, sum1, sum2), (in0, in1, in2)
    pairs = [(sems[2 * i], sems[2 * i + 1]) for i in range(len(sems) // 2)]
    deal_sem, layer_sem, serve_sem, cross_sem, part_sem, back_sem, core_sem, axis_sem, plane_sem = pairs
    me = lax.axis_index("dp")
    where = [place(o, me) for o in range(3)]
    core = me & 1
    barrier = pltpu.get_barrier_semaphore()
    loads = [
        pltpu.make_async_copy(teacher_hbm.at[0], teacher_ref, load_sem.at[0]),
        pltpu.make_async_copy(weight_hbm, weight_ref, load_sem.at[1]),
        pltpu.make_async_copy(nb_hbm, nb_ref, load_sem.at[2]),
        pltpu.make_async_copy(nb_hbm, nbv_ref, load_sem.at[3]),
    ]
    for load in loads:
        load.start()

    for o, step in GREETED:
        layer, spot = where[o]
        pl.semaphore_signal(barrier, inc=1, device_id=(device_at(o, layer, shifted(spot, step)),), device_id_type=MESH)
    loads[0].wait()
    values = unit_rows(teacher_ref[...].astype(jnp.float32))
    unit_ref[...] = values
    wide_ref[:, 768:896] = jnp.transpose(values.astype(jnp.float32)).astype(jnp.bfloat16)
    for load in loads[1:]:
        load.wait()
    pl.semaphore_wait(barrier, len(GREETED))

    def tile(o, spot):
        return wide_ref.at[pl.ds(pl.multiple_of(512 * o + spot * 16, 16), 16), pl.ds(768, 128)]

    own = []
    for o in range(3):
        layer, spot = where[o]

        def deal(step, carry):
            target = shifted(spot, step)
            remote(
                tile(o, target), held[o].at[layer * RING + spot], deal_sem[0].at[o], deal_sem[1].at[o],
                device_at(o, layer, target),
            ).start()
            return carry

        lax.fori_loop(1, RING, deal, 0)
        own.append(pltpu.make_async_copy(tile(o, spot), held[o].at[layer * RING + spot], own_sem.at[o]))
        own[o].start()

    code_unit, inverse = code_rows(dot(unit_ref[...], weight_ref[...]))
    code_ref[...] = code_unit
    inv_ref[...] = jnp.broadcast_to(inverse, inv_ref.shape)

    for o in range(3):
        layer, spot = where[o]
        own[o].wait()
        part = held[o].at[pl.ds(0, RING - 1)]
        remote(part, part, deal_sem[0].at[o], deal_sem[1].at[o], me).wait()
        mine = held[o].at[pl.ds(layer * RING, RING)]
        for hop in range(1, SIDE):
            remote(mine, mine, layer_sem[0].at[o], layer_sem[1].at[o], device_at(o, (layer + hop) & 3, spot)).start()

    units, codes = unit_ref[...], code_ref[...]
    tcorr = dot(units, units, ((1,), (1,)))
    scor = dot(codes, codes, ((1,), (1,)))
    gate = (-(LOSS_SCALE * WEIGHT_SELF) * (tcorr - SHIFT_SELF) * jnp.maximum(scor, 0.0)).astype(jnp.bfloat16)
    self_ref[...] = dot(gate, codes) + dot(gate, codes, ((0,), (0,)))

    for o in range(3):
        layer, spot = where[o]
        part = held[o].at[pl.ds(0, RING * (SIDE - 1))]
        remote(part, part, layer_sem[0].at[o], layer_sem[1].at[o], me).wait()
        rows, cols = pl.ds(pl.multiple_of(512 * o + spot * 16, 16), 16), pl.ds(0, 768)

        def pick(step):
            asker = device_at(o, layer, shifted(spot, step))
            for k in range(KNN):
                up, at = place(o, nb_ref[k, asker])
                picked[o, step, :, 128 * k : 128 * (k + 1)] = held[o][(up << 5) + at]
            return asker

        def serve(step, carry):
            asker = pick(step)
            remote(
                picked.at[o, step], wide_ref.at[rows, cols], serve_sem[0].at[o], serve_sem[1].at[o], asker
            ).start()
            return carry

        lax.fori_loop(1, RING, serve, 0)
        pick(0)
        pltpu.make_async_copy(picked.at[o, 0], wide_ref.at[rows, cols], own_sem.at[o]).start()

    both_ref[0:384, :] = jnp.transpose(weight_ref[...].astype(jnp.float32)).astype(jnp.bfloat16)
    both_ref[384:512, :] = unit_ref[...]
    tcode_ref[...] = jnp.transpose(code_ref[...].astype(jnp.float32)).astype(jnp.bfloat16)
    row = lax.broadcasted_iota(jnp.int32, (768, 768), 0)
    col = lax.broadcasted_iota(jnp.int32, (768, 768), 1)
    perm_ref[...] = jnp.where(
        (row % 24 == ((col >> 7) << 2) + (col & 3)) & (row // 24 == ((col >> 2) & 31)), 1.0, 0.0
    ).astype(jnp.bfloat16)
    row = lax.broadcasted_iota(jnp.int32, (256, 128), 0)
    col = lax.broadcasted_iota(jnp.int32, (256, 128), 1)
    pad_ref[...] = jnp.where(((row >> 3) == (col >> 2)) & ((row & 7) == (col & 3)), 1.0, 0.0).astype(jnp.bfloat16)
    slots = nbv_ref[...].astype(jnp.float32).astype(jnp.bfloat16)
    slot_of = (lax.broadcasted_iota(jnp.int32, (KNN, 768), 1) % 24) >> 2
    mine = slot_of == lax.broadcasted_iota(jnp.int32, (KNN, 768), 0)
    image = lax.broadcasted_iota(jnp.int32, (128, 768), 0)
    source = lax.broadcasted_iota(jnp.int32, (128, 768), 1) // 24
    row = lax.broadcasted_iota(jnp.int32, (512, 768), 0)
    same = (row & 3) == (lax.broadcasted_iota(jnp.int32, (512, 768), 1) & 3)
    for o in range(3):
        layer, spot = where[o]
        chosen = jnp.where(image == device_at(o, layer, source), 1.0, 0.0).astype(jnp.bfloat16)
        named = jnp.sum(jnp.where(mine, dot(slots, chosen), 0.0), axis=0, keepdims=True)
        owner = device_at(o, row >> 7, (row >> 2) & 31).astype(jnp.float32)
        member_ref[o] = jnp.where(same & (owner == named), 1.0, 0.0).astype(jnp.bfloat16)

    for o in range(3):
        pltpu.make_async_copy(picked.at[o, 0], picked.at[o, 0], own_sem.at[o]).wait()
        part = picked.at[o, pl.ds(1, RING - 1)]
        remote(part, part, serve_sem[0].at[o], serve_sem[1].at[o], me).wait()
        third = slice(512 * o, 512 * (o + 1))
        product = dot(both_ref[:, third], wide_ref[third, 0:768])
        product_ref[...] = product if o == 0 else product_ref[...] + product

    values = product_ref[0:384, :].astype(jnp.bfloat16).astype(jnp.float32)
    partner_inv = lax.rsqrt(jnp.sum(values * values, axis=0, keepdims=True) + EPS)
    partner_code = (values * partner_inv).astype(jnp.bfloat16)
    tcorr = product_ref[384:512, :]
    scor = dot(code_ref[...], partner_code)
    gate = (-(LOSS_SCALE * WEIGHT_PAIR) * (tcorr - SHIFT_PAIR) * jnp.maximum(scor, 0.0)).astype(jnp.bfloat16)
    raw = dot(tcode_ref[...], gate)
    values = partner_code.astype(jnp.float32)
    cross = ((raw - values * jnp.sum(values * raw, axis=0, keepdims=True)) * partner_inv).astype(jnp.bfloat16)
    cross_out[...] = dot(perm_ref[...], cross, ((1,), (1,))).reshape(RING, 24, 384).astype(jnp.bfloat16)

    for o in range(3):
        layer, spot = where[o]

        def give(step, carry):
            target = shifted(spot, step)
            remote(
                cross_out.at[target, :, pl.ds(128 * o, 128)], cross_in.at[o, spot], cross_sem[0].at[o], cross_sem[1].at[o],
                device_at(o, layer, target),
            ).start()
            return carry

        lax.fori_loop(1, RING, give, 0)
        cross_in[o, spot] = cross_out[spot, :, 128 * o : 128 * (o + 1)]

    grad = self_ref[...] + dot(gate, partner_code, ((1,), (1,)))
    own_grad = back_norm(grad, code_ref[...], inv_ref[:, 0:1])
    self_ref[...] = own_grad

    coarse = own_grad.astype(jnp.bfloat16)
    fine = (own_grad - coarse.astype(jnp.float32)).astype(jnp.bfloat16)
    share_ref[0:1536, :] = (
        dot(wide_ref[:, 0:768], cross, ((1,), (1,))) + dot(wide_ref[:, 768:896], coarse) + dot(wide_ref[:, 768:896], fine)
    )

    def cut(chip, carry):
        first = share_ref[pl.ds(pl.multiple_of(chip * 24, 8), 16), :].astype(jnp.bfloat16)
        second = share_ref[pl.ds(pl.multiple_of(chip * 24 + 8, 8), 24), :][4:20].astype(jnp.bfloat16)
        for o, at in enumerate(((0, chip >> 4, chip & 15), (chip >> 4, (chip >> 2) & 3, chip & 3), (chip >> 2, chip & 3, 0))):
            share_out[o][0, at[0], at[1], at[2]] = first[:, 128 * o : 128 * (o + 1)]
            share_out[o][1, at[0], at[1], at[2]] = second[:, 128 * o : 128 * (o + 1)]
        return carry

    lax.fori_loop(0, 64, cut, 0)
    for o in range(3):
        remote(share_out[o].at[1 - core], share_mid[o], core_sem[0].at[o], core_sem[1].at[o], me + 1 - 2 * core).start()

    for o in range(3):
        layer, spot = where[o]
        part = cross_in.at[o, pl.ds(0, RING - 1)]
        remote(part, part, cross_sem[0].at[o], cross_sem[1].at[o], me).wait()
        piece = dot(member_ref[o], cross_in[o].reshape(768, 128))
        part_out[o] = piece.astype(jnp.bfloat16).reshape(4, 128, 128)
        for hop in range(1, SIDE):
            to = (layer + hop) & 3
            remote(
                part_out.at[o, to], part_in.at[o, layer], part_sem[0].at[o], part_sem[1].at[o], device_at(o, to, spot)
            ).start()
        part_in[o, layer] = part_out[o, layer]

    for o in range(3):
        layer, spot = where[o]
        remote(share_out[o].at[0], share_mid[o], core_sem[0].at[o], core_sem[1].at[o], me).wait()
        total = share_out[o][core].astype(jnp.float32) + share_mid[o][...].astype(jnp.float32)
        share_sum[o][...] = total.astype(jnp.bfloat16)
        for hop in range(1, SIDE):
            to = (layer + hop) & 3
            remote(
                share_sum[o].at[:, to], layer_in[o].at[layer], axis_sem[0].at[o], axis_sem[1].at[o], device_at(o, to, spot)
            ).start()
        layer_in[o][layer] = share_sum[o][:, layer]
    for o in range(3):
        layer, spot = where[o]
        part = part_in.at[o, pl.ds(0, SIDE - 1)]
        remote(part, part, part_sem[0].at[o], part_sem[1].at[o], me).wait()
        relayed = jnp.sum(part_in[o].astype(jnp.float32), axis=0).astype(jnp.bfloat16)
        back_out[o] = dot(pad_ref[...], relayed).reshape(RING, 8, 128).astype(jnp.bfloat16)

        def give_back(step, carry):
            target = shifted(spot, step)
            remote(
                back_out.at[o, target], back_in.at[o, spot], back_sem[0].at[o], back_sem[1].at[o],
                device_at(o, layer, target),
            ).start()
            return carry

        lax.fori_loop(1, RING, give_back, 0)
        back_in[o, spot] = back_out[o, spot]

    for o in range(3):
        layer, spot = where[o]
        at = spot >> 1
        part = layer_in[o].at[pl.ds(0, SIDE - 1)]
        remote(part, part, axis_sem[0].at[o], axis_sem[1].at[o], me).wait()
        total = jnp.sum(layer_in[o][...].astype(jnp.float32), axis=0)
        plane_out[o] = total.astype(jnp.bfloat16).reshape(16, 16, 128)
        for step in range(1, 16):
            to = digit_sum(at, step)
            remote(
                plane_out.at[o, to], plane_in.at[o, at], plane_sem[0].at[o], plane_sem[1].at[o],
                device_at(o, layer, (to << 1) + core),
            ).start()
        plane_in[o, at] = plane_out[o, at]
    for o in range(3):
        lanes = slice(128 * o, 128 * (o + 1))
        part = back_in.at[o, pl.ds(0, RING - 1)]
        remote(part, part, back_sem[0].at[o], back_sem[1].at[o], me).wait()
        relayed = dot(pad_ref[...], back_in[o].reshape(256, 128), ((0,), (0,)))
        grad_ref[:, lanes] = self_ref[:, lanes] + relayed
    grad_copy = pltpu.make_async_copy(grad_ref, grad_hbm.at[0], load_sem.at[0])
    grad_copy.start()
    for o in range(3):
        part = plane_in.at[o, pl.ds(0, 15)]
        remote(part, part, plane_sem[0].at[o], plane_sem[1].at[o], me).wait()
        total = jnp.sum(plane_in[o].astype(jnp.float32), axis=0)
        head_ref[:, 128 * o : 128 * (o + 1)] = total[0:12]
    grad_copy.wait()


def body(teacher, head_weight, neighbours):
    vmem = pl.BlockSpec(memory_space=pltpu.VMEM)
    hbm = pl.BlockSpec(memory_space=pl.ANY)
    half, full = jnp.bfloat16, jnp.float32
    return pl.pallas_call(
        step_kernel,
        out_shape=(jax.ShapeDtypeStruct((12, 384), full), jax.ShapeDtypeStruct((1, 128, 384), full)),
        in_specs=[hbm, hbm, hbm],
        out_specs=(vmem, hbm),
        scratch_shapes=[
            pltpu.SMEM((KNN, 128), jnp.int32),
            pltpu.VMEM((KNN, 128), jnp.int32),
            pltpu.VMEM((128, 1536), half),
            pltpu.VMEM((1536, 384), half),
            pltpu.VMEM((128, 1536), half),
            pltpu.VMEM((512, 1536), half),
            pltpu.VMEM((128, 384), half),
            pltpu.VMEM((384, 128), half),
            pltpu.VMEM((128, 128), full),
            pltpu.VMEM((128, 384), full),
            pltpu.VMEM((128, 384), full),
            pltpu.VMEM((768, 768), half),
            pltpu.VMEM((256, 128), half),
            pltpu.VMEM((3, 512, 768), half),
        ]
        + [pltpu.VMEM((128, 16, 128), half)] * 3
        + [
            pltpu.VMEM((3, RING, 16, KNN * 128), half),
            pltpu.VMEM((1536, 896), half),
            pltpu.VMEM((512, 768), full),
            pltpu.VMEM((1544, 384), full),
            pltpu.VMEM((RING, 24, 384), half),
            pltpu.VMEM((3, RING, 24, 128), half),
            pltpu.VMEM((3, 4, 128, 128), half),
            pltpu.VMEM((3, 4, 128, 128), half),
            pltpu.VMEM((3, RING, 8, 128), half),
            pltpu.VMEM((3, RING, 8, 128), half),
        ]
        + [pltpu.VMEM((2, a, 4, b, 16, 128), half) for a, b in SPLIT]
        + [pltpu.VMEM((a, 4, b, 16, 128), half) for a, b in SPLIT] * 2
        + [pltpu.VMEM((4, a, b, 16, 128), half) for a, b in SPLIT]
        + [pltpu.VMEM((3, 16, 16, 128), half)] * 2
        + [pltpu.SemaphoreType.DMA((4,)), pltpu.SemaphoreType.DMA((3,))]
        + [pltpu.SemaphoreType.DMA((3,))] * 18,
        compiler_params=pltpu.CompilerParams(
            collective_id=0, has_side_effects=True, vmem_limit_bytes=63 * 2**20
        ),
    )(jnp.transpose(neighbours), teacher, head_weight)


def solution(mesh):
    return jax.shard_map(
        body,
        mesh=mesh,
        in_specs=(P("dp", None, None), P(), P()),
        out_specs=(P("dp", None), P("dp", None, None)),
        check_vma=False,
    )
```

time: 97.9 us -> 75.9 us (0.78)
  Pallas kernels: 92.8 us -> 71.2 us
  local copies, waits for them, and re-layouts: 4.23 us -> 2.96 us
    pallas_call x1, Pallas kernels: 92.8 us -> 71.2 us  [body(): pl.pallas_call(step_kernel, out_shape=(jax.ShapeDtypeStruct((12, 384), fu...]
    unnamed x8 -> x2, local copies, waits for them, and re-layouts: 4.23 us -> 2.96 us
where the time goes in v4:
time: 75.9 us; the launch traced here: 74.8 us
  Pallas kernels  71.2 us (94%)
  local copies, waits for them, and re-layouts  2.96 us (4%)
    pallas_call x1, Pallas kernels, body(): pl.pallas_call(step_kernel, out_shape=(jax.ShapeDtypeStruct((12, 384), fu...  71.2 us
    unnamed x2, local copies, waits for them, and re-layouts  2.96 us

profile of v4, /device:TPU:1, one launch (start us, length us, event | category | flops | bytes accessed | tf_op | source)
XLA Modules:
  0.0 74.8 jit_solution(617957216978932588)
XLA Ops:
  0.6 71.2 %shard_map.50 = (f32[12,384]{1,0:T(8,128)}, f32[1,128,384]{2,1,0:T(8,128)}) custom-call(s32[6,128]{1,0:T(8,128)} %bitcast.1, bf16[1,128,1536]{2,1,0:T(8,128)(2,1)} %teacher_hbm.1, bf16[1536,384]{1,0:T(8,128)(2,1)} %weight_hbm.1), custom_call_target="tpu_custom_call" | custom-call | tf_op jit(solution)/shard_map/pallas_call | solution.py:333
  71.8 1.3 %copy.7 = f32[12,384]{1,0:T(8,128)} copy(f32[12,384]{1,0:T(8,128)} %get-tuple-element.4) | data formatting | bytes 36864
  73.2 1.6 %copy.8 = f32[1,128,384]{2,1,0:T(8,128)} copy(f32[1,128,384]{2,1,0:T(8,128)} %get-tuple-element.5) | data formatting | bytes 393216

commit v5 on v4

v5 whole, which is shorter than its diff:
```python
import jax
import jax.numpy as jnp
from jax import lax
from jax.experimental import pallas as pl
from jax.experimental.pallas import tpu as pltpu
from jax.sharding import PartitionSpec as P

EPS = 1e-06
LOSS_SCALE = 128.0
SHIFT_SELF = 0.18
WEIGHT_SELF = 0.1
SHIFT_PAIR = 0.12
WEIGHT_PAIR = 0.5
MESH = pl.DeviceIdType.MESH
SIDE = 4
RING = 32
KNN = 6


def place(orient, index):
    y, x, z, c = index >> 5, (index >> 3) & 3, (index >> 1) & 3, index & 1
    if orient == 0:
        return y, index & 31
    if orient == 1:
        return x, (y << 3) + (index & 7)
    return z, ((index >> 3) << 1) + c


def device_at(orient, layer, spot):
    if orient == 0:
        return (layer << 5) + spot
    if orient == 1:
        return ((spot >> 3) << 5) + (layer << 3) + (spot & 7)
    return ((spot >> 1) << 3) + (layer << 1) + (spot & 1)


def shifted(spot, step):
    a = ((spot >> 3) + (step >> 3)) & 3
    b = ((spot >> 1) + (step >> 1)) & 3
    return (a << 3) + (b << 1) + ((spot + step) & 1)


def remote(src, dst, send, recv, device):
    return pltpu.make_async_remote_copy(
        src_ref=src, dst_ref=dst, send_sem=send, recv_sem=recv, device_id=(device,), device_id_type=MESH
    )


def unit_rows(values):
    total = jnp.sum(values * values, axis=-1, keepdims=True)
    return (values * lax.rsqrt(total + EPS)).astype(jnp.bfloat16)


def code_rows(codes):
    values = codes.astype(jnp.bfloat16).astype(jnp.float32)
    inverse = lax.rsqrt(jnp.sum(values * values, axis=-1, keepdims=True) + EPS)
    return (values * inverse).astype(jnp.bfloat16), inverse


def back_norm(grad, code_unit, inverse):
    values = code_unit.astype(jnp.float32)
    return (grad - values * jnp.sum(values * grad, axis=-1, keepdims=True)) * inverse


def dot(a, b, dims=((1,), (0,))):
    return lax.dot_general(a, b, (dims, ((), ())), preferred_element_type=jnp.float32)


def digit_sum(place_sum, step):
    return ((((place_sum >> 2) + (step >> 2)) & 3) << 2) + ((place_sum + step) & 3)


SPLIT = ((1, 16), (4, 4), (16, 1))
GREETED = [(0, step) for step in range(1, 32)] + [(1, step) for step in range(8, 32)]
GREETED += [(2, step) for step in range(8, 32) if (step >> 1) & 3]
GREETED.sort(key=lambda at: -(min(at[1] >> 3, 4 - (at[1] >> 3)) + min((at[1] >> 1) & 3, 4 - ((at[1] >> 1) & 3))))


def step_kernel(
    nb_hbm, teacher_hbm, weight_hbm, head_ref, grad_ref,
    table_ref, tablev_ref, nbv_ref, teacher_ref, weight_ref, unit_ref, both_ref, code_ref, tcode_ref, inv_ref, self_ref,
    perm_ref, swap_ref, member_ref, stage, held0, held1, held2, picked, wide_ref, product_ref, share_ref,
    cross_out, cross_in, part_out, part_in,
    out0, out1, out2, mid0, mid1, mid2, sum0, sum1, sum2, in0, in1, in2, tail_out, tail_in,
    load_sem, own_sem, *sems,
):
    held, share_out, share_mid = (held0, held1, held2), (out0, out1, out2), (mid0, mid1, mid2)
    share_sum, layer_in = (sum0, sum1, sum2), (in0, in1, in2)
    pairs = [(sems[2 * i], sems[2 * i + 1]) for i in range(len(sems) // 2)]
    deal_sem, layer_sem, serve_sem, cross_sem, part_sem, core_sem, axis_sem, tail_sem = pairs
    me = lax.axis_index("dp")
    where = [place(o, me) for o in range(3)]
    core = me & 1
    barrier = pltpu.get_barrier_semaphore()
    loads = [
        pltpu.make_async_copy(teacher_hbm.at[0], teacher_ref, load_sem.at[0]),
        pltpu.make_async_copy(weight_hbm, weight_ref, load_sem.at[1]),
        pltpu.make_async_copy(nb_hbm, nbv_ref, load_sem.at[2]),
    ]
    for load in loads:
        load.start()

    for o, step in GREETED:
        layer, spot = where[o]
        pl.semaphore_signal(barrier, inc=1, device_id=(device_at(o, layer, shifted(spot, step)),), device_id_type=MESH)
    loads[0].wait()
    values = unit_rows(teacher_ref[...].astype(jnp.float32))
    unit_ref[...] = values
    wide_ref[:, 768:896] = jnp.transpose(values.astype(jnp.float32)).astype(jnp.bfloat16)
    for load in loads[1:]:
        load.wait()
    named = nbv_ref[...]
    for o in range(3):
        up, at = place(o, named)
        tablev_ref[o, 0:KNN, :] = (up << 5) + ((at & 1) << 4) + (at >> 1)
        tablev_ref[o, KNN:8, :] = jnp.zeros((2, 128), jnp.int32)
    table_load = pltpu.make_async_copy(tablev_ref, table_ref, load_sem.at[3])
    table_load.start()
    table_load.wait()
    pl.semaphore_wait(barrier, len(GREETED))

    def tile(o, at):
        return wide_ref.at[pl.ds(pl.multiple_of(512 * o + at * 32, 32), 32), pl.ds(768, 128)]

    own = []
    for o in range(3):
        layer, spot = where[o]
        at = spot >> 1

        def deal(step, carry):
            to = digit_sum(at, step)
            remote(
                tile(o, to), stage.at[o, at], deal_sem[0].at[o], deal_sem[1].at[o],
                device_at(o, layer, (to << 1) + core),
            ).start()
            return carry

        lax.fori_loop(1, 16, deal, 0)
        own.append(pltpu.make_async_copy(tile(o, at), stage.at[o, at], own_sem.at[o]))
        own[o].start()

    code_unit, inverse = code_rows(dot(unit_ref[...], weight_ref[...]))
    code_ref[...] = code_unit
    inv_ref[...] = jnp.broadcast_to(inverse, inv_ref.shape)

    for o in range(3):
        layer, spot = where[o]
        own[o].wait()
        part = stage.at[o, pl.ds(0, 15)]
        remote(part, part, deal_sem[0].at[o], deal_sem[1].at[o], me).wait()
        mine = held[o].at[pl.ds((layer * 2 + core) * 16, 16)]
        for hop in range(1, 8):
            up, side = (layer + (hop >> 1)) & 3, (core + hop) & 1
            remote(
                stage.at[o, :, pl.ds(pl.multiple_of(side * 16, 16), 16)], mine, layer_sem[0].at[o], layer_sem[1].at[o],
                device_at(o, up, spot - core + side),
            ).start()
        own[o] = pltpu.make_async_copy(stage.at[o, :, pl.ds(pl.multiple_of(core * 16, 16), 16)], mine, own_sem.at[o])
        own[o].start()

    units, codes = unit_ref[...], code_ref[...]
    tcorr = dot(units, units, ((1,), (1,)))
    scor = dot(codes, codes, ((1,), (1,)))
    gate = (-(LOSS_SCALE * WEIGHT_SELF) * (tcorr - SHIFT_SELF) * jnp.maximum(scor, 0.0)).astype(jnp.bfloat16)
    self_ref[...] = dot(gate, codes) + dot(gate, codes, ((0,), (0,)))

    both_ref[0:384, :] = jnp.transpose(weight_ref[...].astype(jnp.float32)).astype(jnp.bfloat16)
    both_ref[384:512, :] = units
    tcode_ref[...] = jnp.transpose(codes.astype(jnp.float32)).astype(jnp.bfloat16)
    row = lax.broadcasted_iota(jnp.int32, (768, 128), 0)
    col = lax.broadcasted_iota(jnp.int32, (768, 128), 1)
    block = (row * 2731) >> 16
    within = jnp.where(block == (col >> 2), row - 24 * block - (col & 3), -1)
    for k in range(KNN):
        perm_ref[:, 128 * k : 128 * (k + 1)] = jnp.where(within == 4 * k, 1.0, 0.0).astype(jnp.bfloat16)
    row = lax.broadcasted_iota(jnp.int32, (128, 128), 0)
    col = lax.broadcasted_iota(jnp.int32, (128, 128), 1)
    swap_ref[...] = jnp.where(
        col == (((row >> 2) & 1) << 6) + ((row >> 3) << 2) + (row & 3), 1.0, 0.0
    ).astype(jnp.bfloat16)

    spans = []
    for o in range(3):
        layer, spot = where[o]
        own[o].wait()
        part = held[o].at[pl.ds(0, 7 * 16)]
        remote(part, part, layer_sem[0].at[o], layer_sem[1].at[o], me).wait()
        spans.append((pl.ds(pl.multiple_of(512 * o + spot * 16, 16), 16), pl.ds(0, 768)))

    def pick(o, step):
        layer, spot = where[o]
        asker = device_at(o, layer, shifted(spot, step))
        for k in range(KNN):
            picked[o, step, :, 128 * k : 128 * (k + 1)] = held[o][table_ref[o, k, asker]]
        return asker

    def serve(step, carry):
        for o in range(3):
            asker = pick(o, step)
            remote(
                picked.at[o, step], wide_ref.at[spans[o][0], spans[o][1]], serve_sem[0].at[o], serve_sem[1].at[o], asker
            ).start()
        return carry

    lax.fori_loop(1, RING, serve, 0)
    for o in range(3):
        pick(o, 0)
        pltpu.make_async_copy(picked.at[o, 0], wide_ref.at[spans[o][0], spans[o][1]], own_sem.at[o]).start()

    slots = nbv_ref[...].astype(jnp.float32).astype(jnp.bfloat16)
    col = lax.broadcasted_iota(jnp.int32, (1, 768), 1)
    source = (col * 2731) >> 16
    slot_of = (col - 24 * source) >> 2
    mine = lax.broadcasted_iota(jnp.int32, (KNN, 768), 0) == slot_of
    image = lax.broadcasted_iota(jnp.int32, (128, 768), 0)
    row = lax.broadcasted_iota(jnp.int32, (512, 128), 0)
    same = (row & 3) == (lax.broadcasted_iota(jnp.int32, (512, 128), 1) & 3)
    for o in range(3):
        layer, spot = where[o]
        chosen = jnp.where(image == device_at(o, layer, source), 1.0, 0.0).astype(jnp.bfloat16)
        named = jnp.sum(jnp.where(mine, dot(slots, chosen), 0.0), axis=0, keepdims=True)
        owner = device_at(o, row >> 7, (((row >> 2) & 15) << 1) + ((row >> 6) & 1))
        owner = jnp.where(same, owner, -1).astype(jnp.float32)
        for k in range(KNN):
            lanes = slice(128 * k, 128 * (k + 1))
            member_ref[o, :, lanes] = jnp.where(owner == named[:, lanes], 1.0, 0.0).astype(jnp.bfloat16)

    for o in range(3):
        pltpu.make_async_copy(picked.at[o, 0], picked.at[o, 0], own_sem.at[o]).wait()
        part = picked.at[o, pl.ds(1, RING - 1)]
        remote(part, part, serve_sem[0].at[o], serve_sem[1].at[o], me).wait()
        third = slice(512 * o, 512 * (o + 1))
        product = dot(both_ref[:, third], wide_ref[third, 0:768])
        product_ref[...] = product if o == 0 else product_ref[...] + product

    values = product_ref[0:384, :].astype(jnp.bfloat16).astype(jnp.float32)
    partner_inv = lax.rsqrt(jnp.sum(values * values, axis=0, keepdims=True) + EPS)
    partner_code = (values * partner_inv).astype(jnp.bfloat16)
    tcorr = product_ref[384:512, :]
    scor = dot(code_ref[...], partner_code)
    gate = (-(LOSS_SCALE * WEIGHT_PAIR) * (tcorr - SHIFT_PAIR) * jnp.maximum(scor, 0.0)).astype(jnp.bfloat16)
    raw = dot(tcode_ref[...], gate)
    values = partner_code.astype(jnp.float32)
    cross = ((raw - values * jnp.sum(values * raw, axis=0, keepdims=True)) * partner_inv).astype(jnp.bfloat16)
    cross_out[...] = dot(perm_ref[...], cross, ((1,), (1,))).reshape(RING, 24, 384).astype(jnp.bfloat16)

    def give(step, carry):
        for o in range(3):
            layer, spot = where[o]
            target = shifted(spot, step)
            remote(
                cross_out.at[target, :, pl.ds(128 * o, 128)], cross_in.at[o, spot], cross_sem[0].at[o], cross_sem[1].at[o],
                device_at(o, layer, target),
            ).start()
        return carry

    lax.fori_loop(1, RING, give, 0)
    for o in range(3):
        spot = where[o][1]
        cross_in[o, spot] = cross_out[spot, :, 128 * o : 128 * (o + 1)]

    grad = self_ref[...] + dot(gate, partner_code, ((1,), (1,)))
    own_grad = back_norm(grad, code_ref[...], inv_ref[:, 0:1])
    self_ref[...] = own_grad

    coarse = own_grad.astype(jnp.bfloat16)
    fine = (own_grad - coarse.astype(jnp.float32)).astype(jnp.bfloat16)
    share_ref[0:1536, :] = (
        dot(wide_ref[:, 0:768], cross, ((1,), (1,))) + dot(wide_ref[:, 768:896], coarse) + dot(wide_ref[:, 768:896], fine)
    )

    def cut(chip, carry):
        first = share_ref[pl.ds(pl.multiple_of(chip * 24, 8), 16), :].astype(jnp.bfloat16)
        second = share_ref[pl.ds(pl.multiple_of(chip * 24 + 8, 8), 24), :][4:20].astype(jnp.bfloat16)
        for o, at in enumerate(((0, chip >> 4, chip & 15), (chip >> 4, (chip >> 2) & 3, chip & 3), (chip >> 2, chip & 3, 0))):
            share_out[o][0, at[0], at[1], at[2]] = first[:, 128 * o : 128 * (o + 1)]
            share_out[o][1, at[0], at[1], at[2]] = second[:, 128 * o : 128 * (o + 1)]
        return carry

    lax.fori_loop(0, 64, cut, 0)
    for o in range(3):
        remote(share_out[o].at[1 - core], share_mid[o], core_sem[0].at[o], core_sem[1].at[o], me + 1 - 2 * core).start()

    for o in range(3):
        layer, spot = where[o]
        remote(share_out[o].at[0], share_mid[o], core_sem[0].at[o], core_sem[1].at[o], me).wait()
        total = share_out[o][core].astype(jnp.float32) + share_mid[o][...].astype(jnp.float32)
        share_sum[o][...] = total.astype(jnp.bfloat16)
        for hop in range(1, SIDE):
            to = (layer + hop) & 3
            remote(
                share_sum[o].at[:, to], layer_in[o].at[layer], axis_sem[0].at[o], axis_sem[1].at[o], device_at(o, to, spot)
            ).start()
        layer_in[o][layer] = share_sum[o][:, layer]

    for o in range(3):
        layer, spot = where[o]
        part = cross_in.at[o, pl.ds(0, RING - 1)]
        remote(part, part, cross_sem[0].at[o], cross_sem[1].at[o], me).wait()
        piece = dot(member_ref[o], cross_in[o].reshape(768, 128))
        part_out[o] = piece.astype(jnp.bfloat16).reshape(8, 64, 128)
        mine = layer * 2 + core
        for hop in range(1, 8):
            up, side = (layer + (hop >> 1)) & 3, (core + hop) & 1
            remote(
                part_out.at[o, up * 2 + side], part_in.at[o, mine], part_sem[0].at[o], part_sem[1].at[o],
                device_at(o, up, spot - core + side),
            ).start()
        part_in[o, mine] = part_out[o, mine]

    for o in range(3):
        layer, spot = where[o]
        at = spot >> 1
        part = part_in.at[o, pl.ds(0, 7)]
        remote(part, part, part_sem[0].at[o], part_sem[1].at[o], me).wait()
        relayed = jnp.sum(part_in[o].reshape(4, 128, 128).astype(jnp.float32), axis=0).astype(jnp.bfloat16)
        tail_out[o, :, 16:24] = dot(swap_ref[...], relayed).reshape(16, 8, 128).astype(jnp.bfloat16)
        part = layer_in[o].at[pl.ds(0, SIDE - 1)]
        remote(part, part, axis_sem[0].at[o], axis_sem[1].at[o], me).wait()
        total = jnp.sum(layer_in[o][...].astype(jnp.float32), axis=0)
        tail_out[o, :, 0:16] = total.astype(jnp.bfloat16).reshape(16, 16, 128)

        def finish(step, carry):
            to = digit_sum(at, step)
            remote(
                tail_out.at[o, to], tail_in.at[o, at], tail_sem[0].at[o], tail_sem[1].at[o],
                device_at(o, layer, (to << 1) + core),
            ).start()
            return carry

        lax.fori_loop(1, 16, finish, 0)
        tail_in[o, at] = tail_out[o, at]

    for o in range(3):
        lanes = slice(128 * o, 128 * (o + 1))
        part = tail_in.at[o, pl.ds(0, 15)]
        remote(part, part, tail_sem[0].at[o], tail_sem[1].at[o], me).wait()
        relayed = tail_in[o, :, 16:24].astype(jnp.float32).reshape(128, 128)
        grad_ref[0, :, lanes] = self_ref[:, lanes] + relayed
        total = jnp.sum(tail_in[o, :, 0:16].astype(jnp.float32), axis=0)
        head_ref[:, lanes] = total[0:12]


def body(teacher, head_weight, neighbours):
    vmem = pl.BlockSpec(memory_space=pltpu.VMEM)
    hbm = pl.BlockSpec(memory_space=pl.ANY)
    half, full = jnp.bfloat16, jnp.float32
    return pl.pallas_call(
        step_kernel,
        out_shape=(jax.ShapeDtypeStruct((12, 384), full), jax.ShapeDtypeStruct((1, 128, 384), full)),
        in_specs=[hbm, hbm, hbm],
        out_specs=(vmem, vmem),
        scratch_shapes=[
            pltpu.SMEM((3, 8, 128), jnp.int32),
            pltpu.VMEM((3, 8, 128), jnp.int32),
            pltpu.VMEM((KNN, 128), jnp.int32),
            pltpu.VMEM((128, 1536), half),
            pltpu.VMEM((1536, 384), half),
            pltpu.VMEM((128, 1536), half),
            pltpu.VMEM((512, 1536), half),
            pltpu.VMEM((128, 384), half),
            pltpu.VMEM((384, 128), half),
            pltpu.VMEM((128, 128), full),
            pltpu.VMEM((128, 384), full),
            pltpu.VMEM((768, 768), half),
            pltpu.VMEM((128, 128), half),
            pltpu.VMEM((3, 512, 768), half),
            pltpu.VMEM((3, 16, 32, 128), half),
        ]
        + [pltpu.VMEM((128, 16, 128), half)] * 3
        + [
            pltpu.VMEM((3, RING, 16, KNN * 128), half),
            pltpu.VMEM((1536, 896), half),
            pltpu.VMEM((512, 768), full),
            pltpu.VMEM((1544, 384), full),
            pltpu.VMEM((RING, 24, 384), half),
            pltpu.VMEM((3, RING, 24, 128), half),
            pltpu.VMEM((3, 8, 64, 128), half),
            pltpu.VMEM((3, 8, 64, 128), half),
        ]
        + [pltpu.VMEM((2, a, 4, b, 16, 128), half) for a, b in SPLIT]
        + [pltpu.VMEM((a, 4, b, 16, 128), half) for a, b in SPLIT] * 2
        + [pltpu.VMEM((4, a, b, 16, 128), half) for a, b in SPLIT]
        + [pltpu.VMEM((3, 16, 24, 128), half)] * 2
        + [pltpu.SemaphoreType.DMA((4,)), pltpu.SemaphoreType.DMA((3,))]
        + [pltpu.SemaphoreType.DMA((3,))] * 16,
        compiler_params=pltpu.CompilerParams(
            collective_id=0, has_side_effects=True, vmem_limit_bytes=(65536 - 10752) * 1024
        ),
    )(jnp.transpose(neighbours), teacher, head_weight)


def solution(mesh):
    return jax.shard_map(
        body,
        mesh=mesh,
        in_specs=(P("dp", None, None), P(), P()),
        out_specs=(P("dp", None), P("dp", None, None)),
        check_vma=False,
    )
```

time: 75.9 us -> 70.8 us (0.933); the launches traced: 74.8 us -> 70.6 us
  Pallas kernels: 71.2 us -> 68 us
  local copies, waits for them, and re-layouts: 2.96 us -> 1.97 us
    pallas_call x1, Pallas kernels: 71.2 us -> 68 us  [body(): pl.pallas_call(step_kernel, out_shape=(jax.ShapeDtypeStruct((12, 384), fu...]
    unnamed x2 -> x4, local copies, waits for them, and re-layouts: 2.96 us -> 1.97 us
where the time goes in v5:
time: 70.8 us; the launch traced here: 70.6 us
  Pallas kernels  68 us (96%)
  local copies, waits for them, and re-layouts  1.97 us (3%)
    pallas_call x1, Pallas kernels, body(): pl.pallas_call(step_kernel, out_shape=(jax.ShapeDtypeStruct((12, 384), fu...  68 us
    unnamed x4, local copies, waits for them, and re-layouts  1.97 us

profile of v5, /device:TPU:1, one launch (start us, length us, event | category | flops | bytes accessed | tf_op | source)
XLA Modules:
  0.0 70.6 jit_solution(10716267894747082112)
XLA Ops:
  0.6 0.0 copy-start
  0.6 0.7 copy-done
  1.3 68.0 %shard_map.50 = (f32[12,384]{1,0:T(8,128)S(1)}, f32[1,128,384]{2,1,0:T(8,128)S(1)}) custom-call(s32[6,128]{1,0:T(8,128)S(1)} %bitcast.1, bf16[1,128,1536]{2,1,0:T(8,128)(2,1)} %teacher_hbm.1, bf16[1536,384]{1,0:T(8,128)(2,1)} %weight_hbm.1), custom_call_target="tpu_custom_call" | custom-call | tf_op jit(solution)/shard_map/pallas_call | solution.py:348
  69.3 0.6 copy.7
  69.9 0.7 copy.8
Async XLA Ops:
  0.6 0.7 copy-start

commit v6 on v5

--- a/solution.py
+++ b/solution.py
@@ -70,6 +70,7 @@
     return ((((place_sum >> 2) + (step >> 2)) & 3) << 2) + ((place_sum + step) & 3)
 
 
+WAVE = 4
 SPLIT = ((1, 16), (4, 4), (16, 1))
 GREETED = [(0, step) for step in range(1, 32)] + [(1, step) for step in range(8, 32)]
 GREETED += [(2, step) for step in range(8, 32) if (step >> 1) & 3]
@@ -79,7 +80,8 @@
 def step_kernel(
     nb_hbm, teacher_hbm, weight_hbm, head_ref, grad_ref,
     table_ref, tablev_ref, nbv_ref, teacher_ref, weight_ref, unit_ref, both_ref, code_ref, tcode_ref, inv_ref, self_ref,
-    perm_ref, swap_ref, member_ref, stage, held0, held1, held2, picked, wide_ref, product_ref, share_ref,
+    perm_ref, swap_ref, member_ref, stage, held0, held1, held2, picked0, picked1, wide0, wide1, tall_ref, product0, product1,
+    mixed_ref, share_ref,
     cross_out, cross_in, part_out, part_in,
     out0, out1, out2, mid0, mid1, mid2, sum0, sum1, sum2, in0, in1, in2, tail_out, tail_in,
     load_sem, own_sem, *sems,
@@ -87,7 +89,11 @@
     held, share_out, share_mid = (held0, held1, held2), (out0, out1, out2), (mid0, mid1, mid2)
     share_sum, layer_in = (sum0, sum1, sum2), (in0, in1, in2)
     pairs = [(sems[2 * i], sems[2 * i + 1]) for i in range(len(sems) // 2)]
-    deal_sem, layer_sem, serve_sem, cross_sem, part_sem, core_sem, axis_sem, tail_sem = pairs
+    deal_sem, layer_sem, serve0_sem, serve1_sem, cross_sem, part_sem, core_sem, axis_sem, tail_sem = pairs
+    waves = (
+        (0, WAVE, picked0, wide0, product0, serve0_sem),
+        (WAVE, KNN, picked1, wide1, product1, serve1_sem),
+    )
     me = lax.axis_index("dp")
     where = [place(o, me) for o in range(3)]
     core = me & 1
@@ -106,7 +112,7 @@
     loads[0].wait()
     values = unit_rows(teacher_ref[...].astype(jnp.float32))
     unit_ref[...] = values
-    wide_ref[:, 768:896] = jnp.transpose(values.astype(jnp.float32)).astype(jnp.bfloat16)
+    tall_ref[...] = jnp.transpose(values.astype(jnp.float32)).astype(jnp.bfloat16)
     for load in loads[1:]:
         load.wait()
     named = nbv_ref[...]
@@ -120,7 +126,7 @@
     pl.semaphore_wait(barrier, len(GREETED))
 
     def tile(o, at):
-        return wide_ref.at[pl.ds(pl.multiple_of(512 * o + at * 32, 32), 32), pl.ds(768, 128)]
+        return tall_ref.at[pl.ds(pl.multiple_of(512 * o + at * 32, 32), 32)]
 
     own = []
     for o in range(3):
@@ -185,27 +191,28 @@
         own[o].wait()
         part = held[o].at[pl.ds(0, 7 * 16)]
         remote(part, part, layer_sem[0].at[o], layer_sem[1].at[o], me).wait()
-        spans.append((pl.ds(pl.multiple_of(512 * o + spot * 16, 16), 16), pl.ds(0, 768)))
-
-    def pick(o, step):
-        layer, spot = where[o]
-        asker = device_at(o, layer, shifted(spot, step))
-        for k in range(KNN):
-            picked[o, step, :, 128 * k : 128 * (k + 1)] = held[o][table_ref[o, k, asker]]
-        return asker
-
-    def serve(step, carry):
+        spans.append(pl.ds(pl.multiple_of(512 * o + spot * 16, 16), 16))
+
+    for first, last, picked, wide, _, sem in waves:
+
+        def pick(o, step):
+            layer, spot = where[o]
+            asker = device_at(o, layer, shifted(spot, step))
+            for k in range(first, last):
+                lanes = slice(128 * (k - first), 128 * (k - first + 1))
+                picked[o, step, :, lanes] = held[o][table_ref[o, k, asker]]
+            return asker
+
+        def serve(step, carry):
+            for o in range(3):
+                asker = pick(o, step)
+                remote(picked.at[o, step], wide.at[spans[o]], sem[0].at[o], sem[1].at[o], asker).start()
+            return carry
+
+        lax.fori_loop(1, RING, serve, 0)
         for o in range(3):
-            asker = pick(o, step)
-            remote(
-                picked.at[o, step], wide_ref.at[spans[o][0], spans[o][1]], serve_sem[0].at[o], serve_sem[1].at[o], asker
-            ).start()
-        return carry
-
-    lax.fori_loop(1, RING, serve, 0)
-    for o in range(3):
-        pick(o, 0)
-        pltpu.make_async_copy(picked.at[o, 0], wide_ref.at[spans[o][0], spans[o][1]], own_sem.at[o]).start()
+            pick(o, 0)
+            pltpu.make_async_copy(picked.at[o, 0], wide.at[spans[o]], own_sem.at[o + (3 if first else 0)]).start()
 
     slots = nbv_ref[...].astype(jnp.float32).astype(jnp.bfloat16)
     col = lax.broadcasted_iota(jnp.int32, (1, 768), 1)
@@ -225,24 +232,31 @@
             lanes = slice(128 * k, 128 * (k + 1))
             member_ref[o, :, lanes] = jnp.where(owner == named[:, lanes], 1.0, 0.0).astype(jnp.bfloat16)
 
-    for o in range(3):
-        pltpu.make_async_copy(picked.at[o, 0], picked.at[o, 0], own_sem.at[o]).wait()
-        part = picked.at[o, pl.ds(1, RING - 1)]
-        remote(part, part, serve_sem[0].at[o], serve_sem[1].at[o], me).wait()
-        third = slice(512 * o, 512 * (o + 1))
-        product = dot(both_ref[:, third], wide_ref[third, 0:768])
-        product_ref[...] = product if o == 0 else product_ref[...] + product
-
-    values = product_ref[0:384, :].astype(jnp.bfloat16).astype(jnp.float32)
-    partner_inv = lax.rsqrt(jnp.sum(values * values, axis=0, keepdims=True) + EPS)
-    partner_code = (values * partner_inv).astype(jnp.bfloat16)
-    tcorr = product_ref[384:512, :]
-    scor = dot(code_ref[...], partner_code)
-    gate = (-(LOSS_SCALE * WEIGHT_PAIR) * (tcorr - SHIFT_PAIR) * jnp.maximum(scor, 0.0)).astype(jnp.bfloat16)
-    raw = dot(tcode_ref[...], gate)
-    values = partner_code.astype(jnp.float32)
-    cross = ((raw - values * jnp.sum(values * raw, axis=0, keepdims=True)) * partner_inv).astype(jnp.bfloat16)
-    cross_out[...] = dot(perm_ref[...], cross, ((1,), (1,))).reshape(RING, 24, 384).astype(jnp.bfloat16)
+    for first, last, picked, wide, product_ref, sem in waves:
+        for o in range(3):
+            pltpu.make_async_copy(picked.at[o, 0], picked.at[o, 0], own_sem.at[o + (3 if first else 0)]).wait()
+            part = picked.at[o, pl.ds(1, RING - 1)]
+            remote(part, part, sem[0].at[o], sem[1].at[o], me).wait()
+            third = slice(512 * o, 512 * (o + 1))
+            product = dot(both_ref[:, third], wide[third, :])
+            product_ref[...] = product if o == 0 else product_ref[...] + product
+
+        values = product_ref[0:384, :].astype(jnp.bfloat16).astype(jnp.float32)
+        partner_inv = lax.rsqrt(jnp.sum(values * values, axis=0, keepdims=True) + EPS)
+        partner_code = (values * partner_inv).astype(jnp.bfloat16)
+        tcorr = product_ref[384:512, :]
+        scor = dot(code_ref[...], partner_code)
+        gate = (-(LOSS_SCALE * WEIGHT_PAIR) * (tcorr - SHIFT_PAIR) * jnp.maximum(scor, 0.0)).astype(jnp.bfloat16)
+        raw = dot(tcode_ref[...], gate)
+        values = partner_code.astype(jnp.float32)
+        cross = ((raw - values * jnp.sum(values * raw, axis=0, keepdims=True)) * partner_inv).astype(jnp.bfloat16)
+        mixed = dot(perm_ref[:, 128 * first : 128 * last], cross, ((1,), (1,)))
+        if first == 0:
+            mixed_ref[...] = mixed
+            self_ref[...] = self_ref[...] + dot(gate, partner_code, ((1,), (1,)))
+            share_ref[0:1536, :] = dot(wide[...], cross, ((1,), (1,)))
+        else:
+            cross_out[...] = (mixed_ref[...] + mixed).reshape(RING, 24, 384).astype(jnp.bfloat16)
 
     def give(step, carry):
         for o in range(3):
@@ -265,8 +279,8 @@
 
     coarse = own_grad.astype(jnp.bfloat16)
     fine = (own_grad - coarse.astype(jnp.float32)).astype(jnp.bfloat16)
-    share_ref[0:1536, :] = (
-        dot(wide_ref[:, 0:768], cross, ((1,), (1,))) + dot(wide_ref[:, 768:896], coarse) + dot(wide_ref[:, 768:896], fine)
+    share_ref[0:1536, :] = share_ref[0:1536, :] + (
+        dot(wide1[...], cross, ((1,), (1,))) + dot(tall_ref[...], coarse) + dot(tall_ref[...], fine)
     )
 
     def cut(chip, carry):
@@ -369,9 +383,14 @@
         ]
         + [pltpu.VMEM((128, 16, 128), half)] * 3
         + [
-            pltpu.VMEM((3, RING, 16, KNN * 128), half),
-            pltpu.VMEM((1536, 896), half),
-            pltpu.VMEM((512, 768), full),
+            pltpu.VMEM((3, RING, 16, WAVE * 128), half),
+            pltpu.VMEM((3, RING, 16, (KNN - WAVE) * 128), half),
+            pltpu.VMEM((1536, WAVE * 128), half),
+            pltpu.VMEM((1536, (KNN - WAVE) * 128), half),
+            pltpu.VMEM((1536, 128), half),
+            pltpu.VMEM((512, WAVE * 128), full),
+            pltpu.VMEM((512, (KNN - WAVE) * 128), full),
+            pltpu.VMEM((768, 384), full),
             pltpu.VMEM((1544, 384), full),
             pltpu.VMEM((RING, 24, 384), half),
             pltpu.VMEM((3, RING, 24, 128), half),
@@ -382,8 +401,8 @@
         + [pltpu.VMEM((a, 4, b, 16, 128), half) for a, b in SPLIT] * 2
         + [pltpu.VMEM((4, a, b, 16, 128), half) for a, b in SPLIT]
         + [pltpu.VMEM((3, 16, 24, 128), half)] * 2
-        + [pltpu.SemaphoreType.DMA((4,)), pltpu.SemaphoreType.DMA((3,))]
-        + [pltpu.SemaphoreType.DMA((3,))] * 16,
+        + [pltpu.SemaphoreType.DMA((4,)), pltpu.SemaphoreType.DMA((6,))]
+        + [pltpu.SemaphoreType.DMA((3,))] * 18,
         compiler_params=pltpu.CompilerParams(
             collective_id=0, has_side_effects=True, vmem_limit_bytes=(65536 - 10752) * 1024
         ),

time: 70.8 us -> 67.2 us (0.949)
  Pallas kernels: 68 us -> 64.4 us
    pallas_call x1, Pallas kernels: 68 us -> 64.4 us  [body(): pl.pallas_call(step_kernel, out_shape=(jax.ShapeDtypeStruct((12, 384), fu...]
where the time goes in v6:
time: 67.2 us; the launch traced here: 67.1 us
  Pallas kernels  64.4 us (96%)
  local copies, waits for them, and re-layouts  1.97 us (3%)
    pallas_call x1, Pallas kernels, body(): pl.pallas_call(step_kernel, out_shape=(jax.ShapeDtypeStruct((12, 384), fu...  64.4 us
    unnamed x4, local copies, waits for them, and re-layouts  1.97 us

profile of v6, /device:TPU:1, one launch (start us, length us, event | category | flops | bytes accessed | tf_op | source)
XLA Modules:
  0.0 67.1 jit_solution(3369208094953298697)
XLA Ops:
  0.6 0.0 copy-start
  0.6 0.7 %copy-done = s32[128,6]{0,1:T(8,128)S(1)} copy-done((s32[128,6]{0,1:T(8,128)S(1)}, s32[128,6]{0,1:T(8,128)}, u32[]{:S(2)}) %copy-start) | copy-done | bytes 3096
  1.3 64.4 %shard_map.50 = (f32[12,384]{1,0:T(8,128)S(1)}, f32[1,128,384]{2,1,0:T(8,128)S(1)}) custom-call(s32[6,128]{1,0:T(8,128)S(1)} %bitcast.1, bf16[1,128,1536]{2,1,0:T(8,128)(2,1)} %teacher_hbm.1, bf16[1536,384]{1,0:T(8,128)(2,1)} %weight_hbm.1), custom_call_target="tpu_custom_call" | custom-call | tf_op jit(solution)/shard_map/pallas_call | solution.py:362
  65.8 0.6 copy.7
  66.4 0.7 %copy.8 = f32[1,128,384]{2,1,0:T(8,128)} copy(f32[1,128,384]{2,1,0:T(8,128)S(1)} %get-tuple-element.5) | data formatting | bytes 393216
Async XLA Ops:
  0.6 0.7 %copy-start = (s32[128,6]{0,1:T(8,128)S(1)}, s32[128,6]{0,1:T(8,128)}, u32[]{:S(2)}) copy-start(s32[128,6]{0,1:T(8,128)} %param.5) | copy-start | bytes 9220

commit v7 on v6

--- a/solution.py
+++ b/solution.py
@@ -71,6 +71,8 @@
 
 
 WAVE = 4
+FAR1 = sorted(range(1, 16), key=lambda step: -(min(step >> 2, 4 - (step >> 2)) + min(step & 3, 4 - (step & 3))))
+FAR2 = sorted(range(1, 32), key=lambda step: -(min(step >> 3, 4 - (step >> 3)) + min((step >> 1) & 3, 4 - ((step >> 1) & 3))))
 SPLIT = ((1, 16), (4, 4), (16, 1))
 GREETED = [(0, step) for step in range(1, 32)] + [(1, step) for step in range(8, 32)]
 GREETED += [(2, step) for step in range(8, 32) if (step >> 1) & 3]
@@ -141,7 +143,8 @@
             ).start()
             return carry
 
-        lax.fori_loop(1, 16, deal, 0)
+        for step in FAR1:
+            deal(step, 0)
         own.append(pltpu.make_async_copy(tile(o, at), stage.at[o, at], own_sem.at[o]))
         own[o].start()
 
@@ -155,7 +158,7 @@
         part = stage.at[o, pl.ds(0, 15)]
         remote(part, part, deal_sem[0].at[o], deal_sem[1].at[o], me).wait()
         mine = held[o].at[pl.ds((layer * 2 + core) * 16, 16)]
-        for hop in range(1, 8):
+        for hop in (4, 5, 2, 3, 6, 7, 1):
             up, side = (layer + (hop >> 1)) & 3, (core + hop) & 1
             remote(
                 stage.at[o, :, pl.ds(pl.multiple_of(side * 16, 16), 16)], mine, layer_sem[0].at[o], layer_sem[1].at[o],
@@ -268,7 +271,8 @@
             ).start()
         return carry
 
-    lax.fori_loop(1, RING, give, 0)
+    for step in FAR2:
+        give(step, 0)
     for o in range(3):
         spot = where[o][1]
         cross_in[o, spot] = cross_out[spot, :, 128 * o : 128 * (o + 1)]
@@ -283,16 +287,18 @@
         dot(wide1[...], cross, ((1,), (1,))) + dot(tall_ref[...], coarse) + dot(tall_ref[...], fine)
     )
 
-    def cut(chip, carry):
-        first = share_ref[pl.ds(pl.multiple_of(chip * 24, 8), 16), :].astype(jnp.bfloat16)
-        second = share_ref[pl.ds(pl.multiple_of(chip * 24 + 8, 8), 24), :][4:20].astype(jnp.bfloat16)
-        for o, at in enumerate(((0, chip >> 4, chip & 15), (chip >> 4, (chip >> 2) & 3, chip & 3), (chip >> 2, chip & 3, 0))):
-            share_out[o][0, at[0], at[1], at[2]] = first[:, 128 * o : 128 * (o + 1)]
-            share_out[o][1, at[0], at[1], at[2]] = second[:, 128 * o : 128 * (o + 1)]
-        return carry
-
-    lax.fori_loop(0, 64, cut, 0)
-    for o in range(3):
+    for o in range(3):
+        lanes = slice(128 * o, 128 * (o + 1))
+
+        def cut(chip, carry):
+            a, b, c = ((0, chip >> 4, chip & 15), (chip >> 4, (chip >> 2) & 3, chip & 3), (chip >> 2, chip & 3, 0))[o]
+            first = share_ref[pl.ds(pl.multiple_of(chip * 24, 8), 16), lanes]
+            second = share_ref[pl.ds(pl.multiple_of(chip * 24 + 8, 8), 24), lanes][4:20]
+            share_out[o][0, a, b, c] = first.astype(jnp.bfloat16)
+            share_out[o][1, a, b, c] = second.astype(jnp.bfloat16)
+            return carry
+
+        lax.fori_loop(0, 64, cut, 0)
         remote(share_out[o].at[1 - core], share_mid[o], core_sem[0].at[o], core_sem[1].at[o], me + 1 - 2 * core).start()
 
     for o in range(3):
@@ -300,7 +306,7 @@
         remote(share_out[o].at[0], share_mid[o], core_sem[0].at[o], core_sem[1].at[o], me).wait()
         total = share_out[o][core].astype(jnp.float32) + share_mid[o][...].astype(jnp.float32)
         share_sum[o][...] = total.astype(jnp.bfloat16)
-        for hop in range(1, SIDE):
+        for hop in (2, 1, 3):
             to = (layer + hop) & 3
             remote(
                 share_sum[o].at[:, to], layer_in[o].at[layer], axis_sem[0].at[o], axis_sem[1].at[o], device_at(o, to, spot)
@@ -314,7 +320,7 @@
         piece = dot(member_ref[o], cross_in[o].reshape(768, 128))
         part_out[o] = piece.astype(jnp.bfloat16).reshape(8, 64, 128)
         mine = layer * 2 + core
-        for hop in range(1, 8):
+        for hop in (4, 5, 2, 3, 6, 7, 1):
             up, side = (layer + (hop >> 1)) & 3, (core + hop) & 1
             remote(
                 part_out.at[o, up * 2 + side], part_in.at[o, mine], part_sem[0].at[o], part_sem[1].at[o],
@@ -342,7 +348,8 @@
             ).start()
             return carry
 
-        lax.fori_loop(1, 16, finish, 0)
+        for step in FAR1:
+            finish(step, 0)
         tail_in[o, at] = tail_out[o, at]
 
     for o in range(3):

time: 67.2 us -> 65.4 us (0.973)
  Pallas kernels: 64.4 us -> 62.6 us
    pallas_call x1, Pallas kernels: 64.4 us -> 62.6 us  [body(): pl.pallas_call(step_kernel, out_shape=(jax.ShapeDtypeStruct((12, 384), fu...]
where the time goes in v7:
time: 65.4 us; the launch traced here: 65.3 us
  Pallas kernels  62.6 us (96%)
  local copies, waits for them, and re-layouts  1.97 us (3%)
    pallas_call x1, Pallas kernels, body(): pl.pallas_call(step_kernel, out_shape=(jax.ShapeDtypeStruct((12, 384), fu...  62.6 us
    unnamed x4, local copies, waits for them, and re-layouts  1.97 us

profile of v7, /device:TPU:1, one launch (start us, length us, event | category | flops | bytes accessed | tf_op | source)
XLA Modules:
  0.0 65.3 jit_solution(6176708391539099585)
XLA Ops:
  0.6 0.0 copy-start
  0.6 0.7 %copy-done = s32[128,6]{0,1:T(8,128)S(1)} copy-done((s32[128,6]{0,1:T(8,128)S(1)}, s32[128,6]{0,1:T(8,128)}, u32[]{:S(2)}) %copy-start) | copy-done | bytes 3096
  1.3 62.6 %shard_map.50 = (f32[12,384]{1,0:T(8,128)S(1)}, f32[1,128,384]{2,1,0:T(8,128)S(1)}) custom-call(s32[6,128]{1,0:T(8,128)S(1)} %bitcast.1, bf16[1,128,1536]{2,1,0:T(8,128)(2,1)} %teacher_hbm.1, bf16[1536,384]{1,0:T(8,128)(2,1)} %weight_hbm.1), custom_call_target="tpu_custom_call" | custom-call | tf_op jit(solution)/shard_map/pallas_call | solution.py:369
  64.0 0.6 copy.7
  64.6 0.7 %copy.8 = f32[1,128,384]{2,1,0:T(8,128)} copy(f32[1,128,384]{2,1,0:T(8,128)S(1)} %get-tuple-element.5) | data formatting | bytes 393216
Async XLA Ops:
  0.6 0.7 %copy-start = (s32[128,6]{0,1:T(8,128)S(1)}, s32[128,6]{0,1:T(8,128)}, u32[]{:S(2)}) copy-start(s32[128,6]{0,1:T(8,128)} %param.5) | copy-start | bytes 9220

commit v8 on v7

--- a/solution.py
+++ b/solution.py
@@ -212,7 +212,8 @@
                 remote(picked.at[o, step], wide.at[spans[o]], sem[0].at[o], sem[1].at[o], asker).start()
             return carry
 
-        lax.fori_loop(1, RING, serve, 0)
+        lax.fori_loop(20, RING, serve, 0)
+        lax.fori_loop(1, 20, serve, 0)
         for o in range(3):
             pick(o, 0)
             pltpu.make_async_copy(picked.at[o, 0], wide.at[spans[o]], own_sem.at[o + (3 if first else 0)]).start()
@@ -287,19 +288,22 @@
         dot(wide1[...], cross, ((1,), (1,))) + dot(tall_ref[...], coarse) + dot(tall_ref[...], fine)
     )
 
-    for o in range(3):
+    def cut_side(o, side):
         lanes = slice(128 * o, 128 * (o + 1))
 
         def cut(chip, carry):
             a, b, c = ((0, chip >> 4, chip & 15), (chip >> 4, (chip >> 2) & 3, chip & 3), (chip >> 2, chip & 3, 0))[o]
-            first = share_ref[pl.ds(pl.multiple_of(chip * 24, 8), 16), lanes]
-            second = share_ref[pl.ds(pl.multiple_of(chip * 24 + 8, 8), 24), lanes][4:20]
-            share_out[o][0, a, b, c] = first.astype(jnp.bfloat16)
-            share_out[o][1, a, b, c] = second.astype(jnp.bfloat16)
+            rows = share_ref[pl.ds(pl.multiple_of(chip * 24, 8), 32), lanes]
+            share_out[o][side, a, b, c] = jnp.where(side == 0, rows[0:16], rows[12:28]).astype(jnp.bfloat16)
             return carry
 
-        lax.fori_loop(0, 64, cut, 0)
+        lax.fori_loop(0, 64, cut, 0, unroll=4)
+
+    for o in range(3):
+        cut_side(o, 1 - core)
         remote(share_out[o].at[1 - core], share_mid[o], core_sem[0].at[o], core_sem[1].at[o], me + 1 - 2 * core).start()
+    for o in range(3):
+        cut_side(o, core)
 
     for o in range(3):
         layer, spot = where[o]

time: 65.4 us -> 65 us (level)
  no operation moved by 1% of the time
where the time goes in v8:
time: 65 us; the launch traced here: 64.9 us
  Pallas kernels  62.2 us (96%)
  local copies, waits for them, and re-layouts  1.97 us (3%)
  between operations  0.65 us (1%)
    pallas_call x1, Pallas kernels, body(): pl.pallas_call(step_kernel, out_shape=(jax.ShapeDtypeStruct((12, 384), fu...  62.2 us
    unnamed x4, local copies, waits for them, and re-layouts  1.97 us

profile of v8, /device:TPU:1, one launch (start us, length us, event | category | flops | bytes accessed | tf_op | source)
XLA Modules:
  0.0 64.9 jit_solution(3065774796534178182)
XLA Ops:
  0.6 0.0 copy-start
  0.6 0.7 %copy-done = s32[128,6]{0,1:T(8,128)S(1)} copy-done((s32[128,6]{0,1:T(8,128)S(1)}, s32[128,6]{0,1:T(8,128)}, u32[]{:S(2)}) %copy-start) | copy-done | bytes 3096
  1.3 62.2 %shard_map.50 = (f32[12,384]{1,0:T(8,128)S(1)}, f32[1,128,384]{2,1,0:T(8,128)S(1)}) custom-call(s32[6,128]{1,0:T(8,128)S(1)} %bitcast.1, bf16[1,128,1536]{2,1,0:T(8,128)(2,1)} %teacher_hbm.1, bf16[1536,384]{1,0:T(8,128)(2,1)} %weight_hbm.1), custom_call_target="tpu_custom_call" | custom-call | tf_op jit(solution)/shard_map/pallas_call | solution.py:373
  63.6 0.6 copy.7
  64.2 0.7 %copy.8 = f32[1,128,384]{2,1,0:T(8,128)} copy(f32[1,128,384]{2,1,0:T(8,128)S(1)} %get-tuple-element.5) | data formatting | bytes 393216
Async XLA Ops:
  0.6 0.7 %copy-start = (s32[128,6]{0,1:T(8,128)S(1)}, s32[128,6]{0,1:T(8,128)}, u32[]{:S(2)}) copy-start(s32[128,6]{0,1:T(8,128)} %param.5) | copy-start | bytes 9220
